TPU v7x, 128 devices: a whole 4x4x4 slice. The times are simulated.
128 devices in a mesh: row: 8 (over y, x_lo), col: 16 (over z, x_hi, core).
Axes of the slice: x: 4 (x_hi: 2, x_lo: 2; x = x_hi * 2 + x_lo), y: 4, z: 4, core: 2. Of those that a mesh axis runs over, the one named last changes fastest.
Arguments:
- image: bfloat16 [128, 512, 256], P('row', 'col'), may hold values from -6 to 6
- na_qkv: bfloat16 [256, 768], replicated, as said below
- na_out: bfloat16 [256, 256], replicated, may hold values from -0.375 to 0.375
- merge_one: bfloat16 [1024, 512], replicated, may hold values from -0.1875 to 0.1875
- merge_two: bfloat16 [2048, 1024], replicated, may hold values from -0.125 to 0.125
- attn_qkv: bfloat16 [1024, 3072], replicated, as said below
- attn_out: bfloat16 [1024, 1024], replicated, may hold values from -0.1875 to 0.1875
- cotangent: bfloat16 [32, 128, 1024], P('row', 'col'), may hold values from -6 to 6
Outputs:
- merged_out: bfloat16 [32, 128, 1024], P('row', 'col')
- grad_image: bfloat16 [128, 512, 256], P('row', 'col')
- grad_attn_out: float32 [1024, 1024], P(('row', 'col'))
Inputs may be any that keep to these rules, and one draw needn't show every extreme that they name: `na_qkv`: columns hold the query, key and value projections in this order, each split into heads of consecutive columns. `attn_qkv`: columns hold the query, key and value projections in this order, each split into heads of consecutive columns.
All inputs are finite; a program needn't handle non-finite values.
Results may differ from a plain program's by a relative error of at most 0.027.
Values may be sent and summed in bfloat16 or wider, within the bound.
No kernel may reach another device: no remote copies, remote signals or barrier semaphores. Data moves between devices by JAX's collectives and lax.ppermute only.
A program may use at most 128 MiB of HBM per device.

v0:
```python
import functools
import math

import jax
import jax.numpy as jnp
import numpy as np
from jax import lax
from jax.experimental import pallas as pl
from jax.experimental.pallas import tpu as pltpu
from jax.sharding import PartitionSpec as P

C0 = 256
C1 = 512
C2 = 1024
NA_HEADS = 4
GHEADS = 8
KERNEL = 7
REACH = KERNEL // 2
EPSILON = 1e-06
LANES = 128
NA_DIM = C0 // NA_HEADS
WIDE = NA_HEADS * LANES
MASKED = -1e15
ROWS = 16
DELTA_LANE = 112
LSE_LANE = 114

f32 = jnp.float32
bf16 = jnp.bfloat16


def dot(left, right):
    return lax.dot_general(left, right, (((1,), (0,)), ((), ())), preferred_element_type=f32)


def dot_last(left, right):
    return lax.dot_general(left, right, (((1,), (1,)), ((), ())), preferred_element_type=f32)


def dot_first(left, right):
    return lax.dot_general(left, right, (((0,), (0,)), ((), ())), preferred_element_type=f32)


def rms_stat(x):
    return lax.rsqrt(jnp.mean(x * x, -1, keepdims=True) + EPSILON)


def rms_back(x, scale, grad):
    return scale * grad - x * scale**3 * jnp.mean(grad * x, -1, keepdims=True)


def token_tables(rows, cols):
    grid = np.arange(rows * cols).reshape(rows // 4, 2, 2, cols // 4, 2, 2)
    order = grid.transpose(2, 5, 1, 4, 0, 3).reshape(-1)
    own_row, own_col = order // cols, order % cols
    outside = [(-99, -99)]
    side = [
        ((r0, r1), pad)
        for (r0, r1), pad in [((-REACH, 0), True), ((0, rows), False), ((rows, rows + REACH), True)]
    ]
    halo = [(r, c) for r in range(-REACH, 0) for c in range(cols)]
    halo += [(r, c) for r in range(rows, rows + REACH) for c in range(cols)]
    for first in (-REACH, cols):
        for (r0, r1), pad in side:
            part = [(r, c) for r in range(r0, r1) for c in range(first, first + REACH)]
            halo += part + outside * (-len(part) % ROWS)
    count = len(halo)
    padded = -(-count // LANES) * LANES
    halo = np.array(halo + outside * (padded - count))

    def band(row, col):
        near_row = np.abs(row[:, None] - np.arange(rows)[None]) <= REACH
        near_col = np.abs(col[:, None] - np.arange(cols)[None]) <= REACH
        return np.where(np.concatenate([near_row, near_col], 1), 0.0, MASKED)

    def lanes(part):
        table = np.zeros((part.shape[0], LANES), np.float32)
        table[:, NA_DIM : NA_DIM + part.shape[1]] = part
        return table

    hot = np.concatenate(
        [own_row[:, None] == np.arange(rows)[None], own_col[:, None] == np.arange(cols)[None]], 1
    ).astype(np.float32)
    perm = np.zeros((rows * cols, rows * cols), np.float32)
    perm[np.arange(rows * cols), order] = 1.0
    place = np.argsort(order)
    natural = np.arange(rows * cols).reshape(rows, cols)
    strips = [natural[:REACH], natural[-REACH:], natural[:, :REACH], natural[:, -REACH:]]
    wanted = place[np.concatenate([s.reshape(-1) for s in strips])]
    select = np.zeros((wanted.size, rows * cols), np.float32)
    select[np.arange(wanted.size), wanted] = 1.0
    corner = np.zeros((2 * ROWS, REACH * cols), np.float32)
    for i, first in enumerate((0, cols - REACH)):
        for r in range(REACH):
            for c in range(REACH):
                corner[i * ROWS + r * REACH + c, r * cols + first + c] = 1.0
    return dict(
        corner=corner,
        perm=perm,
        select=select,
        hot=lanes(hot),
        band_own=lanes(band(own_row, own_col)),
        band_halo=lanes(band(halo[:, 0], halo[:, 1])),
        halo=halo,
        count=count,
    )


def shifted(array, axis, move):
    count = lax.axis_size(axis)
    return lax.ppermute(array, axis, [(i, move(i)) for i in range(count)])


def neighbours(to_next, to_previous, axis):
    count = lax.axis_size(axis)
    up = [(i, i + 1) for i in range(count - 1)]
    down = [(j, i) for i, j in up]
    return lax.ppermute(to_next, axis, up), lax.ppermute(to_previous, axis, down)


def row_halo(top, bottom):
    return neighbours(bottom, top, "row")


def along_z(pair):
    count = lax.axis_size("col")
    return [pair] + [shifted(pair, "col", lambda i: (i + 4 * step) % count) for step in (1, 3, 2)]


def other_core(pieces):
    return [shifted(piece, "col", lambda i: i ^ 1) for piece in pieces]


def across(shard):
    return shifted(shard, "col", lambda i: i ^ 2)


def column_order():
    count = lax.axis_size("col")
    place = jnp.arange(count, dtype=jnp.int32)
    step = jnp.asarray([0, 1, 3, 2], jnp.int32)[place % 4]
    source = (lax.axis_index("col") + count - 4 * step) % count
    return source ^ (2 * ((place // 4) % 2)) ^ (place // 8)


def all_to_all(array, axis):
    return lax.all_to_all(array, axis, split_axis=0, concat_axis=0, tiled=True)


class Rows:
    def __init__(self, array, rows):
        self.array, self.rows = array, rows
        self.shape, self.dtype = (rows, *array.shape[1:]), array.dtype


class Held:
    def __init__(self, source, target, sems, cut):
        dim, count = cut
        size = target.shape[dim] // count
        self.copies = []
        self.parts = []
        for i in range(count):
            at = tuple(pl.ds(i * size, size) if d == dim else slice(None) for d in range(dim + 1))
            part = target.at[at] if count > 1 else target
            self.copies.append(
                pltpu.make_async_copy(source.at[at] if count > 1 else source, part, sems[i])
            )
            self.parts.append(part)
        self.target = target
        self.waiting = [True] * count
        for copy in self.copies:
            copy.start()

    def chunk(self, i):
        if self.waiting[i]:
            self.waiting[i] = False
            self.copies[i].wait()
        return self.parts[i]

    def ready(self):
        for i in range(len(self.copies)):
            self.chunk(i)
        return self.target

    def __getitem__(self, index):
        return self.ready()[index]

    @property
    def shape(self):
        return self.target.shape


class Plain:
    def __init__(self, target):
        self.target = target

    def ready(self):
        return self.target

    def send(self):
        pass

    def __getitem__(self, index):
        return self.target[index]

    def __setitem__(self, index, value):
        self.target[index] = value

    @property
    def shape(self):
        return self.target.shape


class Result(Plain):
    def __init__(self, source, target, sem):
        self.copy = pltpu.make_async_copy(source, target, sem)
        self.target = source
        self.started = False

    def send(self):
        if not self.started:
            self.started = True
            self.copy.start()


def take_from(items, count):
    return [items.pop(0) for _ in range(count)]


def call(kernel, outs, args, manual=(), out_manual=(), scratch=(), smem=0, cuts={}, megabytes=16):
    manual = sorted(i % len(args) for i in manual)
    out_manual = sorted(i % len(outs) for i in out_manual)
    cuts = {i % len(args): cut for i, cut in cuts.items()}
    cuts = [cuts.get(i, (0, 1)) for i in manual]
    total = sum(n for _, n in cuts)

    def body(*refs):
        refs = list(refs)
        take = functools.partial(take_from, refs)
        given, results, extra = take(len(args)), take(len(outs)), take(len(scratch))
        here, there = take(len(manual)), take(len(out_manual))
        sems_in, sems_out = take(2)
        sems = [sems_in.at[i] for i in range(total)]
        values = given[:smem] + [Plain(ref) for ref in given[smem:]]
        writes = [Plain(ref) for ref in results]
        for i, dst, cut in zip(manual, here, cuts):
            source = given[i].at[pl.ds(0, args[i].rows)] if isinstance(args[i], Rows) else given[i]
            values[i] = Held(source, dst, take_from(sems, cut[1]), cut)
        for n, (i, src) in enumerate(zip(out_manual, there)):
            writes[i] = Result(src, results[i], sems_out.at[n])
        kernel(*values, *writes, *extra)
        for i in out_manual:
            writes[i].send()
        for i in manual:
            values[i].ready()
        for i in out_manual:
            writes[i].copy.wait()

    def spec(i, far):
        return pl.BlockSpec(memory_space=pltpu.HBM if i in far else pltpu.VMEM)

    hbm = lambda a: pltpu.with_memory_space_constraint(a, pltpu.HBM)
    return pl.pallas_call(
        body,
        out_shape=[
            pltpu.HBM(*out) if i in out_manual else jax.ShapeDtypeStruct(*out)
            for i, out in enumerate(outs)
        ],
        in_specs=[pl.BlockSpec(memory_space=pltpu.SMEM)] * smem
        + [spec(i, manual) for i in range(smem, len(args))],
        out_specs=[spec(i, out_manual) for i in range(len(outs))],
        scratch_shapes=list(scratch)
        + [pltpu.VMEM(args[i].shape, args[i].dtype) for i in manual]
        + [pltpu.VMEM(*outs[i]) for i in out_manual]
        + [pltpu.SemaphoreType.DMA((max(total, 1),)), pltpu.SemaphoreType.DMA((max(len(out_manual), 1),))],
        compiler_params=pltpu.CompilerParams(vmem_limit_bytes=megabytes * 2**20),
    )(*[hbm(getattr(a, "array", a)) if i in manual else a for i, a in enumerate(args)])


def head_lanes(head):
    return slice(head * LANES, (head + 1) * LANES)


def two_parts(value):
    high = value.astype(bf16).astype(f32)
    return high, value - high


def at_lanes(base, lane, first, value):
    high, low = two_parts(value)
    return jnp.where(lane == first, -high, jnp.where(lane == first + 1, -low, base))


def head_of(pairs, head, section=0):
    first = section * C0 + (head // 2) * LANES
    pair = pairs[:, first : first + LANES]
    return pltpu.roll(pair, NA_DIM, 1) if head % 2 else pair


def as_pairs(heads):
    lane = lax.broadcasted_iota(jnp.int32, (1, LANES), 1)
    pairs = [
        jnp.where(lane < NA_DIM, heads[i], pltpu.roll(heads[i + 1], NA_DIM, 1))
        for i in range(0, len(heads), 2)
    ]
    return jnp.concatenate(pairs, 1).astype(bf16)


def fill_halo(target, parts):
    first = 0
    for part in parts:
        rows = part.shape[0]
        target[first : first + rows, :] = part[...]
        first += rows
    rest = target.shape[0] - first
    target[first:, :] = jnp.zeros((rest, target.shape[1]), target.dtype)


def corner_kernel(corner_ref, before_ref, after_ref, left_ref, right_ref, left_out, right_out):
    for i, (side, out) in enumerate([(left_ref, left_out), (right_ref, right_out)]):
        pick = corner_ref[i * ROWS : (i + 1) * ROWS]
        rows = side.shape[0]
        out[:ROWS] = dot(pick, before_ref[...]).astype(bf16)
        out[ROWS : ROWS + rows] = side[...]
        out[ROWS + rows :] = dot(pick, after_ref[...]).astype(bf16)


def na_forward_kernel(
    x_ref,
    perm_ref,
    w_ref,
    before_ref,
    after_ref,
    left_ref,
    right_ref,
    hot_ref,
    band_own_ref,
    band_halo_ref,
    w_out_ref,
    one_ref,
    two_ref,
    wqkv_ref,
    dout_ref,
    head_out,
    m2_out,
    x_out,
    q_one,
    q_two,
    k_one,
    k_two,
    v_one,
    v_two,
    q_halo_out,
    a0_out,
    halo_ref,
):
    own = x_ref.shape[0]
    x = dot(perm_ref[...], x_ref[...])
    x_out[...] = x.astype(bf16)
    x_out.send()
    xn = (x * rms_stat(x)).astype(bf16)
    fill_halo(halo_ref, [before_ref, after_ref, left_ref, right_ref])
    xh = halo_ref[...].astype(f32)
    xhn = (xh * rms_stat(xh)).astype(bf16)
    mine = dot(xn, w_ref[...])
    beside = dot(xhn, w_ref[...])
    lane = lax.broadcasted_iota(jnp.int32, (1, LANES), 1)
    is_lse = (lane == LSE_LANE) | (lane == LSE_LANE + 1)
    is_delta = (lane == DELTA_LANE) | (lane == DELTA_LANE + 1)
    one_lse = jnp.where(is_lse, 1.0, 0.0)
    one_delta = jnp.where(is_delta, 1.0, 0.0)
    hot = hot_ref[...].astype(f32)
    band_own = band_own_ref[...].astype(f32) + one_lse
    band_halo = band_halo_ref[...].astype(f32)
    channel = lane < NA_DIM
    scale = 1.0 / math.sqrt(NA_DIM)
    outs = []
    for h in range(NA_HEADS):
        at = head_lanes(h)
        to = head_lanes(h % 2)
        q_out, k_out, v_out = (q_two, k_two, v_two) if h // 2 else (q_one, k_one, v_one)
        q = jnp.where(channel, head_of(mine, h) * scale, hot)
        k_out[:own, to] = jnp.where(channel, head_of(mine, h, 1), band_own).astype(bf16)
        k_out[own:, to] = jnp.where(channel, head_of(beside, h, 1), band_halo + one_lse).astype(bf16)
        v_out[:own, to] = jnp.where(channel, head_of(mine, h, 2), one_delta).astype(bf16)
        v_out[own:, to] = jnp.where(channel, head_of(beside, h, 2), one_delta).astype(bf16)
        q_halo_out[:, at] = jnp.where(channel, head_of(beside, h) * scale, band_halo).astype(bf16)
        score = dot_last(q.astype(bf16), k_out[:, to])
        top = jnp.max(score, -1, keepdims=True)
        weight = jnp.exp(score - top).astype(bf16)
        out = dot(weight, v_out[:, to])
        norm = out[:, DELTA_LANE : DELTA_LANE + 1]
        q_out[:, to] = at_lanes(q, lane, LSE_LANE, top + jnp.log(norm)).astype(bf16)
        out = jnp.where(channel, out / norm, 0.0)
        a0_out[:, at] = out.astype(bf16)
        outs.append(out)
    for result in (q_one, q_two, k_one, k_two, v_one, v_two, q_halo_out, a0_out):
        result.send()
    y = (x + dot(as_pairs(outs), w_out_ref[...])).astype(bf16)
    quarter = own // 4
    m1 = dot(y[:quarter], one_ref[:C0])
    for part in range(1, 4):
        m1 += dot(y[part * quarter : (part + 1) * quarter], one_ref[part * C0 : (part + 1) * C0])
    m1 = m1.astype(bf16)
    tokens = own // 16
    m2 = dot(m1[:tokens], two_ref[:C1])
    for part in range(1, 4):
        m2 += dot(m1[part * tokens : (part + 1) * tokens], two_ref[part * C1 : (part + 1) * C1])
    m2 = m2.astype(bf16)
    m2_out[...] = m2
    m2f = m2.astype(f32)
    mn = (m2f * rms_stat(m2f)).astype(bf16)
    dim = C2 // GHEADS
    for part, place in enumerate((2, 0, 1, 3)):
        if part < 3:
            value = dot(mn, wqkv_ref.chunk(part)[...]).astype(bf16)
        else:
            value = dout_ref[...]
        for h in range(GHEADS):
            head_out[h, :, place * dim : (place + 1) * dim] = value[:, h * dim : (h + 1) * dim]


def attention_kernel(scale, grad_ref, query_ref, *refs):
    pieces, (out_ref, col_ref, send_ref) = refs[:-3], refs[-3:]
    owned, dim = out_ref.shape
    query, dout = query_ref[:owned, :dim], query_ref[:owned, dim:]
    scores = [dot_last(query, piece[:, :dim]) * scale for piece in pieces]
    top = functools.reduce(jnp.maximum, [jnp.max(s, -1, keepdims=True) for s in scores])
    norm, out = 0.0, 0.0
    for score, piece in zip(scores, pieces):
        weight = jnp.exp(score - top)
        norm += jnp.sum(weight, -1, keepdims=True)
        out += dot(weight.astype(bf16), piece[:, dim:])
    out = (out / norm).astype(bf16)
    out_ref[...] = out
    lse = top + jnp.log(norm)
    delta = jnp.sum(dout.astype(f32) * out.astype(f32), -1, keepdims=True)
    lane = lax.broadcasted_iota(jnp.int32, (1, LANES), 1)
    col_ref[...] = jnp.where(lane == 0, lse, jnp.where(lane == 1, delta, 0.0))
    parts = [*two_parts(lse), *two_parts(delta)]
    table = jnp.zeros((query.shape[0], LANES), f32)
    for i, part in enumerate(parts):
        table = jnp.where(lane == i, part, table)
    table = table.T
    halves = query.shape[0] // LANES
    stats = [
        table[i : i + 1, half * LANES : (half + 1) * LANES]
        for i in range(len(parts))
        for half in range(halves)
    ]
    stats = jnp.concatenate(stats, 0).astype(bf16)
    partial = dot_first(out, grad_ref[...])
    count, rows = send_ref.shape[0], send_ref.shape[1]
    for i in range(count):
        send_ref[i, :, :C2] = partial[i * rows : (i + 1) * rows].astype(bf16)
        send_ref[i, :, C2:] = stats


def query_grad_kernel(scale, col_ref, query_ref, *refs):
    pieces, dq_ref = refs[:-1], refs[-1]
    owned, dim = dq_ref.shape
    query, dout = query_ref[:owned, :dim], query_ref[:owned, dim:]
    lse, delta = col_ref[:, 0:1], col_ref[:, 1:2]
    total = 0.0
    for piece in pieces:
        keys = piece[:, :dim]
        prob = jnp.exp(dot_last(query, keys) * scale - lse)
        dprob = dot_last(dout, piece[:, dim:])
        total += dot((prob * (dprob - delta)).astype(bf16), keys)
    dq_ref[...] = (total * scale).astype(bf16)


def key_grad_kernel(scale, order_ref, stat_ref, dq_ref, heads_ref, pair_ref, *refs):
    pieces, (out_ref, lse_in, delta_in) = refs[:-3], refs[-3:]
    owned, dim = dq_ref.shape
    halves = owned // LANES
    keys, values = pair_ref[:owned, :dim], pair_ref[:owned, dim:]
    stat_ref = stat_ref.ready()
    dk, dv = 0.0, 0.0
    for i, piece in enumerate(pieces):
        each = piece.shape[0] // owned
        for j in range(each):
            stats = stat_ref[order_ref[each * i + j]][:, C2:].astype(f32)
            for half in range(halves):
                at = slice(j * owned + half * LANES, j * owned + (half + 1) * LANES)
                take = lambda n: stats[n * halves + half : n * halves + half + 1]
                lse_in[:, at] = take(0) + take(1)
                delta_in[:, at] = take(2) + take(3)
        queries, douts = piece[:, :dim], piece[:, dim:]
        prob = jnp.exp(dot_last(keys, queries) * scale - lse_in[...])
        dprob = dot_last(values, douts)
        dk += dot((prob * (dprob - delta_in[...])).astype(bf16), queries)
        dv += dot(prob.astype(bf16), douts)
    out_ref[:, :dim] = dq_ref[...]
    out_ref[:, dim : 2 * dim] = (dk * scale).astype(bf16)
    out_ref[:, 2 * dim : 3 * dim] = dv.astype(bf16)
    out_ref[:, 3 * dim :] = heads_ref[...]


def merge_back_kernel(
    dqkv_ref,
    wqkv_ref,
    m2_ref,
    grad_ref,
    two_ref,
    one_ref,
    w_out_ref,
    a0_ref,
    q_one,
    q_two,
    select_ref,
    dout_out,
    dy_out,
    *strip_outs,
):
    dim = C2 // GHEADS
    dmn = 0.0
    for part in range(3):
        at = slice(part * dim, (part + 1) * dim)
        grads = jnp.concatenate([dqkv_ref[h, :, at] for h in range(GHEADS)], 1)
        dmn += dot_last(grads, wqkv_ref.chunk(part)[...])
    m2 = m2_ref[...].astype(f32)
    dm2 = (grad_ref[...].astype(f32) + rms_back(m2, rms_stat(m2), dmn)).astype(bf16)
    dm1 = [dot_last(dm2, two_ref.chunk(part)[...]).astype(bf16) for part in range(4)]
    du1 = dot_last(jnp.concatenate(dm1, 0), one_ref[...]).astype(bf16)
    dy = jnp.concatenate([du1[:, part * C0 : (part + 1) * C0] for part in range(4)], 0)
    dy_out[...] = dy
    da0 = dot_last(dy, w_out_ref[...]).astype(bf16).astype(f32)
    lane = lax.broadcasted_iota(jnp.int32, (1, LANES), 1)
    is_lse = (lane == LSE_LANE) | (lane == LSE_LANE + 1)
    for h in range(NA_HEADS):
        at = head_lanes(h)
        mine = jnp.where(lane < NA_DIM, head_of(da0, h), 0.0)
        delta = jnp.sum(mine * a0_ref[:, at].astype(f32), -1, keepdims=True)
        q_ref = q_two if h // 2 else q_one
        mine = jnp.where(is_lse, q_ref[:, head_lanes(h % 2)].astype(f32), mine)
        dout_out[:, at] = at_lanes(mine, lane, DELTA_LANE, delta).astype(bf16)
    dout_out.send()
    strips = dot(select_ref[...], dout_out[...]).astype(bf16)
    first = 0
    for out in strip_outs:
        out[...] = strips[first : first + out.shape[0]]
        first += out.shape[0]


def through_projection(grads, section, first, w_ref):
    start = section * C0 + first * NA_DIM
    return dot_last(as_pairs(grads), w_ref[:, start : start + len(grads) * NA_DIM])


def na_own_kernel(heads, q_ref, k_ref, dout_ref, v_ref, w_ref, dxn_out):
    own = dout_ref.shape[0]
    dq, dk, dv = [], [], []
    for i, h in enumerate(heads):
        at = head_lanes(i)
        dout = dout_ref[:, head_lanes(h)]
        prob = jnp.exp(dot_last(q_ref[:, at], k_ref[:, at]))
        dprob = dot_last(dout, v_ref[:, at])
        dscore = (prob * dprob).astype(bf16)
        dq.append(dot(dscore, k_ref[:, at]) * (1.0 / math.sqrt(NA_DIM)))
        dk.append(dot_first(dscore[:, :own], q_ref[:, at]))
        dv.append(dot_first(prob[:, :own].astype(bf16), dout))
    dxn = through_projection(dq, 0, heads[0], w_ref)
    dxn += through_projection(dk, 1, heads[0], w_ref)
    dxn_out[...] = dxn + through_projection(dv, 2, heads[0], w_ref)


def na_rest_kernel(
    heads,
    q_ref,
    k_ref,
    dout_ref,
    v_ref,
    w_ref,
    heads_ref,
    wo_ref,
    m2_ref,
    dxn_out,
    merged_out,
):
    na_own_kernel(heads, q_ref, k_ref, dout_ref, v_ref, w_ref, dxn_out)
    merged = m2_ref[...].astype(f32)
    dim = C2 // GHEADS
    for h in range(GHEADS):
        merged += dot(heads_ref[h, :, 3 * dim :], wo_ref[h * dim : (h + 1) * dim])
    merged_out[...] = merged.astype(bf16)


def na_beside_kernel(
    k_one,
    v_one,
    k_two,
    v_two,
    hot_ref,
    before_ref,
    after_ref,
    left_ref,
    right_ref,
    q_halo_ref,
    w_ref,
    x_ref,
    dxn_one,
    dxn_two,
    dy_ref,
    perm_back_ref,
    grad_out,
    dout_halo_ref,
):
    lane = lax.broadcasted_iota(jnp.int32, (1, LANES), 1)
    is_mask = (lane >= NA_DIM) & (lane < DELTA_LANE)
    is_lse = (lane == LSE_LANE) | (lane == LSE_LANE + 1)
    fill_halo(dout_halo_ref, [before_ref, after_ref, left_ref, right_ref])
    hot = hot_ref[...].astype(f32)
    dk, dv = [], []
    for h in range(NA_HEADS):
        at = head_lanes(h)
        to = head_lanes(h % 2)
        k_ref, v_ref = (k_two, v_two) if h // 2 else (k_one, v_one)
        keys = jnp.where(is_mask, hot, k_ref[:, to].astype(f32)).astype(bf16)
        douts = dout_halo_ref[:, at]
        queries = jnp.where(
            is_lse, douts.astype(f32), q_halo_ref[:, at].astype(f32)
        ).astype(bf16)
        prob = jnp.exp(dot_last(keys, queries))
        dprob = dot_last(v_ref[:, to], douts)
        dk.append(dot((prob * dprob).astype(bf16), queries))
        dv.append(dot(prob.astype(bf16), douts))
    dxn = dxn_one[...] + dxn_two[...] + through_projection(dk, 1, 0, w_ref)
    dxn += through_projection(dv, 2, 0, w_ref)
    x = x_ref[...].astype(f32)
    grad = (dy_ref[...].astype(f32) + rms_back(x, rms_stat(x), dxn)).astype(bf16)
    grad_out[...] = dot(perm_back_ref[...], grad).astype(bf16)


def per_device(image, na_qkv, na_out, merge_one, merge_two, attn_qkv, attn_out, cotangent):
    rows, cols, _ = image.shape
    n_row = lax.axis_size("row")
    n_col = lax.axis_size("col")
    own = rows * cols
    tokens = own // 16
    dim = C2 // GHEADS
    owned = n_row * tokens
    scale = 1.0 / math.sqrt(dim)
    tables = token_tables(rows, cols)
    perm = jnp.asarray(tables["perm"], bf16)
    perm_back = jnp.asarray(tables["perm"].T, bf16)
    select = jnp.asarray(tables["select"], bf16)
    hot = jnp.asarray(tables["hot"], bf16)
    corner = jnp.asarray(tables["corner"], bf16)
    band_own = jnp.asarray(tables["band_own"], bf16)
    halo = tables["halo"]
    padded = halo.shape[0]

    flat = image.reshape(own, C0)
    before, after = row_halo(image[:REACH].reshape(-1, C0), image[-REACH:].reshape(-1, C0))
    left, right = call(
        corner_kernel,
        [((REACH * rows + 2 * ROWS, C0), bf16)] * 2,
        (
            corner,
            before,
            after,
            image[:, :REACH].reshape(-1, C0),
            image[:, -REACH:].reshape(-1, C0),
        ),
        megabytes=8,
    )
    left, right = neighbours(right, left, "col")
    at_row = lax.axis_index("row") * rows + jnp.asarray(halo[:, 0], jnp.int32)
    at_col = lax.axis_index("col") * cols + jnp.asarray(halo[:, 1], jnp.int32)
    inside = (at_row >= 0) & (at_row < rows * n_row) & (at_col >= 0) & (at_col < cols * n_col)
    lane = jnp.arange(LANES)
    mask_lane = (lane >= NA_DIM) & (lane < NA_DIM + rows + cols)
    band_halo = jnp.where(
        ~inside[:, None] & mask_lane[None], MASKED, jnp.asarray(tables["band_halo"], f32)
    ).astype(bf16)

    grad = cotangent.reshape(tokens, C2)
    dout = dot_last(grad, attn_out).astype(bf16)

    heads, m2, xp, q_one, q_two, k_one, k_two, v_one, v_two, q0_halo, a0 = call(
        na_forward_kernel,
        [
            ((GHEADS, tokens, 4 * dim), bf16),
            ((tokens, C2), bf16),
            ((own, C0), bf16),
            ((own, WIDE // 2), bf16),
            ((own, WIDE // 2), bf16),
            ((own + padded, WIDE // 2), bf16),
            ((own + padded, WIDE // 2), bf16),
            ((own + padded, WIDE // 2), bf16),
            ((own + padded, WIDE // 2), bf16),
            ((padded, WIDE), bf16),
            ((own, WIDE), bf16),
        ],
        (
            flat,
            perm,
            na_qkv,
            before,
            after,
            left,
            right,
            hot,
            band_own,
            band_halo,
            na_out,
            merge_one,
            merge_two,
            attn_qkv,
            dout,
        ),
        manual=(0, 1, 2, 7, 8, 9, 10, 11, 12, 13),
        cuts={13: (1, 3)},
        out_manual=range(1, 11),
        scratch=(pltpu.VMEM((padded, C0), bf16),),
        megabytes=40,
    )

    mine = all_to_all(heads, "row").reshape(owned, 4 * dim)
    keyval, queries = mine[:, : 2 * dim], mine[:, 2 * dim :]
    keyval = jnp.concatenate([keyval, across(keyval)], 0)
    queries = jnp.concatenate(along_z(queries), 0)
    keyval, share = lax.optimization_barrier((keyval, grad))
    share = jnp.broadcast_to(share[None], (n_row, tokens, C2))
    grad_row = all_to_all(share, "row").reshape(owned, C2)
    keyval = along_z(keyval)
    keyval_core = other_core(keyval)
    queries = [queries, across(queries)]
    keyval += keyval_core
    out_heads, stats, send = call(
        functools.partial(attention_kernel, scale),
        [((owned, dim), bf16), ((owned, LANES), f32), ((n_col, dim // n_col, C2 + LANES), bf16)],
        (grad_row, queries[0], *keyval),
    )
    shares = all_to_all(send, "col")
    dq = call(
        functools.partial(query_grad_kernel, scale),
        [((owned, dim), bf16)],
        (stats, queries[0], *keyval),
    )[0]
    queries += other_core(queries)
    part = queries[0].shape[0]
    back = call(
        functools.partial(key_grad_kernel, scale),
        [((owned, 4 * dim), bf16)],
        (column_order(), shares, dq, out_heads, keyval[0], *queries),
        scratch=(pltpu.VMEM((1, part), f32), pltpu.VMEM((1, part), f32)),
        smem=1,
    )[0]
    grad_wo = jnp.sum(shares[:, :, :C2].astype(f32), 0)
    back = all_to_all(back.reshape(n_row, tokens, 4 * dim), "row")

    dout0, dy0, top, bottom, left, right = call(
        merge_back_kernel,
        [((own, WIDE), bf16), ((own, C0), bf16)]
        + [((REACH * n, WIDE), bf16) for n in (cols, cols, rows, rows)],
        (back, attn_qkv, m2, grad, merge_two, merge_one, na_out, a0, q_one, q_two, select),
        manual=range(1, 11),
        out_manual=(1,),
        cuts={1: (1, 3), 4: (0, 4)},
        megabytes=32,
    )
    before, after = row_halo(top, bottom)
    half = NA_HEADS // 2
    dxn_one = call(
        functools.partial(na_own_kernel, range(half)),
        [((own, C0), f32)],
        (q_one, k_one, dout0, v_one, na_qkv),
        manual=(0, 1, 3, 4),
    )[0]
    before, after, dxn_one = lax.optimization_barrier((before, after, dxn_one))
    left, right = call(
        corner_kernel,
        [((left.shape[0] + 2 * ROWS, WIDE), bf16)] * 2,
        (corner, before, after, left, right),
        megabytes=8,
    )
    left, right, q_two = lax.optimization_barrier((left, right, q_two))
    left, right = neighbours(right, left, "col")
    dxn_two, merged = call(
        functools.partial(na_rest_kernel, range(half, NA_HEADS)),
        [((own, C0), f32), ((tokens, C2), bf16)],
        (q_two, k_two, dout0, v_two, na_qkv, back, attn_out, m2),
        manual=(0, 1, 3, 4, 6, 7),
        megabytes=20,
    )
    grad_image = call(
        na_beside_kernel,
        [((own, C0), bf16)],
        (
            Rows(k_one, own),
            Rows(v_one, own),
            Rows(k_two, own),
            Rows(v_two, own),
            hot,
            before,
            after,
            left,
            right,
            q0_halo,
            na_qkv,
            xp,
            dxn_one,
            dxn_two,
            dy0,
            perm_back,
        ),
        manual=(0, 1, 2, 3, 4, 9, 10, 11, 14, 15),
        scratch=(pltpu.VMEM((padded, WIDE), bf16),),
    )[0]
    return (
        merged.reshape(rows // 4, cols // 4, C2),
        grad_image.reshape(rows, cols, C0),
        grad_wo,
    )


def solution(mesh):
    return jax.shard_map(
        per_device,
        mesh=mesh,
        in_specs=(P("row", "col", None), P(), P(), P(), P(), P(), P(), P("row", "col", None)),
        out_specs=(P("row", "col", None), P("row", "col", None), P(("row", "col"), None)),
        check_vma=False,
    )
```

profile of v0, /device:TPU:34, one launch (start us, length us, event | category | flops | bytes accessed | tf_op | source)
XLA Modules:
  0.0 147.3 jit_solution(1480436551521101544)
XLA Ops:
  1.5 3.4 %collective-permute-start = (bf16[96,256]{1,0:T(8,128)(2,1)S(1)}, bf16[96,256]{1,0:T(8,128)(2,1)S(1)}, u32[]{:S(2)}, u32[]{:S(2)}) collective-permute-start(bf16[96,256]{1,0:T(8,128)(2,1)S(1)} %bitcast.22), channel_id=1, source_target_pairs={{0,16},{16,32},{32,48},{48,64},{64,80},{80,96},{96,112},{1,17},{17... | collective-permute-start | bytes 147464 | tf_op jit(solution)/shard_map/ppermute | solution.py:118
  5.0 2.4 %collective-permute-start.1 = (bf16[96,256]{1,0:T(8,128)(2,1)S(1)}, bf16[96,256]{1,0:T(8,128)(2,1)S(1)}, u32[]{:S(2)}, u32[]{:S(2)}) collective-permute-start(bf16[96,256]{1,0:T(8,128)(2,1)S(1)} %bitcast.21), channel_id=1, source_target_pairs={{16,0},{32,16},{48,32},{64,48},{80,64},{96,80},{112,96},{17,1},{33... | collective-permute-start | bytes 147464 | tf_op jit(solution)/shard_map/ppermute | solution.py:118
  8.3 2.3 %convolution_convert_fusion.refs_14_ = bf16[32,1024]{1,0:T(8,128)(2,1)S(1)} fusion(bf16[1024,1024]{1,0:T(8,128)(2,1)} %refs_6_.3, bf16[4,8,1024]{2,1,0:T(8,128)(2,1)} %param.25), kind=kOutput, calls=%fused_computation.1 | convolution fusion | flops 67141632 | bytes 2228224 | tf_op jit(solution)/shard_map/dot_general | solution.py:37
  10.8 1.1 collective-permute-done.1.refs_2_.refs_4_
  12.1 1.9 %collective-permute-start.2 = (bf16[80,256]{1,0:T(8,128)(2,1)S(1)}, bf16[80,256]{1,0:T(8,128)(2,1)S(1)}, u32[]{:S(2)}, u32[]{:S(2)}) collective-permute-start(bf16[80,256]{1,0:T(8,128)(2,1)S(1)} %get-tuple-element.37), channel_id=1, source_target_pairs={{0,1},{1,2},{2,3},{3,4},{4,5},{5,6},{6,7},{7,8},{8,9},{9,10},{10,1... | collective-permute-start | bytes 122888 | tf_op jit(solution)/shard_map/ppermute | solution.py:118
  14.0 6.0 %collective-permute-start.3 = (bf16[80,256]{1,0:T(8,128)(2,1)S(1)}, bf16[80,256]{1,0:T(8,128)(2,1)S(1)}, u32[]{:S(2)}, u32[]{:S(2)}) collective-permute-start(bf16[80,256]{1,0:T(8,128)(2,1)S(1)} %get-tuple-element.38), channel_id=1, source_target_pairs={{1,0},{2,1},{3,2},{4,3},{5,4},{6,5},{7,6},{8,7},{9,8},{10,9},{11,1... | collective-permute-start | bytes 122888 | tf_op jit(solution)/shard_map/ppermute | solution.py:118
  21.7 9.7 %shard_map.194 = (bf16[8,32,512]{2,1,0:T(8,128)(2,1)S(1)}, bf16[32,1024]{1,0:T(8,128)(2,1)}, bf16[512,256]{1,0:T(8,128)(2,1)}, bf16[512,256]{1,0:T(8,128)(2,1)},...) custom-call(bf16[512,256]{1,0:T(8,128)(2,1)} %bitcast.17, ...), custom_call_target="tpu_custom_call" | custom-call | tf_op jit(solution)/shard_map/pallas_call | solution.py:263
  31.4 12.8 %all_to_all.20 = bf16[8,32,512]{2,1,0:T(8,128)(2,1)S(1)} all-to-all(bf16[8,32,512]{2,1,0:T(8,128)(2,1)S(1)} %get-tuple-element.39), channel_id=1, replica_groups=mesh['row'=8,'col'=16] {'row'}, dimensions={0} | all-to-all | bytes 524288 | tf_op jit(solution)/shard_map/all_to_all | solution.py:147
  44.2 3.1 %collective-permute-start.7 = (bf16[256,256]{1,0:T(8,128)(2,1)S(1)}, bf16[256,256]{1,0:T(8,128)(2,1)S(1)}, u32[]{:S(2)}, u32[]{:S(2)}) collective-permute-start(bf16[256,256]{1,0:T(8,128)(2,1)S(1)} %get-tuple-element.71), channel_id=1, source_target_pairs={{0,8},{1,9},{2,10},{3,11},{4,12},{5,13},{6,14},{7,15},{8,0},{9,1},... | collective-permute-start | bytes 393224 | tf_op jit(solution)/shard_map/ppermute | solution.py:111
  48.2 1.0 collective-permute-start.5
  49.7 2.4 %collective-permute-done.7 = bf16[256,256]{1,0:T(8,128)(2,1)S(1)} collective-permute-done((bf16[256,256]{1,0:T(8,128)(2,1)S(1)}, bf16[256,256]{1,0:T(8,128)(2,1)S(1)}, u32[]{:S(2)}, u32[]{:S(2)}) %collective-permute-start.7) | collective-permute-done | bytes 131104 | tf_op jit(solution)/shard_map/ppermute | solution.py:111
  52.1 2.0 %collective-permute-done.6 = bf16[256,256]{1,0:T(8,128)(2,1)S(1)} collective-permute-done((bf16[256,256]{1,0:T(8,128)(2,1)S(1)}, bf16[256,256]{1,0:T(8,128)(2,1)S(1)}, u32[]{:S(2)}, u32[]{:S(2)}) %collective-permute-start.6) | collective-permute-done | bytes 131104 | tf_op jit(solution)/shard_map/ppermute | solution.py:111
  55.8 1.7 %collective-permute-start.8 = (bf16[512,256]{1,0:T(8,128)(2,1)S(1)}, bf16[512,256]{1,0:T(8,128)(2,1)S(1)}, u32[]{:S(2)}, u32[]{:S(2)}) collective-permute-start(bf16[512,256]{1,0:T(8,128)(2,1)S(1)} %pad_maximum_fusion.1.refs_2_.refs_4_), channel_id=1, source_target_pairs={{0,4},{1,5},{2,6},{3,7},{4,8},{5,9},{6,10},{7,11},{8,12},{9,13},{1... | collective-permute-start | bytes 786440 | tf_op jit(solution)/shard_map/ppermute | solution.py:111
  57.9 1.8 %collective-permute-start.10 = (bf16[512,256]{1,0:T(8,128)(2,1)S(1)}, bf16[512,256]{1,0:T(8,128)(2,1)S(1)}, u32[]{:S(2)}, u32[]{:S(2)}) collective-permute-start(bf16[512,256]{1,0:T(8,128)(2,1)S(1)} %pad_maximum_fusion.1.refs_2_.refs_4_), channel_id=1, source_target_pairs={{0,8},{1,9},{2,10},{3,11},{4,12},{5,13},{6,14},{7,15},{8,0},{9,1},... | collective-permute-start | bytes 786440 | tf_op jit(solution)/shard_map/ppermute | solution.py:111
  60.5 4.7 %all-to-all-start.1 = ((bf16[8,32,1024]{2,1,0:T(8,128)(2,1)}), bf16[8,32,1024]{2,1,0:T(8,128)(2,1)S(1)}, u32[]{:S(2)}, u32[]{:S(2)}) async-start(bf16[8,32,1024]{2,1,0:T(8,128)(2,1)} %broadcast_in_dim.7), calls=%async_computation.1 | async-start | bytes 1048576 | tf_op jit(solution)/shard_map/all_to_all | solution.py:147
  65.7 1.0 collective-permute-done.9.refs_4_
  66.7 4.2 %collective-permute-done.10.refs_5_ = bf16[512,256]{1,0:T(8,128)(2,1)S(1)} collective-permute-done((bf16[512,256]{1,0:T(8,128)(2,1)S(1)}, bf16[512,256]{1,0:T(8,128)(2,1)S(1)}, u32[]{:S(2)}, u32[]{:S(2)}) %collective-permute-start.10) | collective-permute-done | bytes 262176 | tf_op jit(solution)/shard_map/ppermute | solution.py:111
  71.7 3.7 %all-to-all-done.1 = bf16[8,32,1024]{2,1,0:T(8,128)(2,1)S(1)} async-done(((bf16[8,32,1024]{2,1,0:T(8,128)(2,1)}), bf16[8,32,1024]{2,1,0:T(8,128)(2,1)S(1)}, u32[]{:S(2)}, u32[]{:S(2)}) %all-to-all-start.1) | async-done | bytes 524320 | tf_op jit(solution)/shard_map/all_to_all | solution.py:147
  75.4 3.1 %shard_map.195 = (bf16[256,128]{1,0:T(8,128)(2,1)S(1)}, f32[256,128]{1,0:T(8,128)S(1)}, bf16[16,8,1152]{2,1,0:T(8,128)(2,1)}) custom-call(bf16[256,1024]{1,0:T(8,128)(2,1)S(1)} %bitcast.14, bf16[1024,256]{1,0:T(8,128)(2,1)S(1)} %pad_maximum_fusion.refs_1_.refs_5_, bf16[512,256]{1,0:T(8,128)(2,1)S(1)} %pad_maximum_fusion.1.refs_2_.refs_4_, ...), custom_call_target="tpu_custom_call" | custom-call | tf_op jit(solution)/shard_map/pallas_call | solution.py:263
  78.4 5.2 %all-to-all-start.2 = ((bf16[16,8,1152]{2,1,0:T(8,128)(2,1)}), bf16[16,8,1152]{2,1,0:T(8,128)(2,1)S(1)}, u32[]{:S(2)}, u32[]{:S(2)}) async-start(bf16[16,8,1152]{2,1,0:T(8,128)(2,1)} %get-tuple-element.42), calls=%async_computation.2 | async-start | bytes 589824 | tf_op jit(solution)/shard_map/all_to_all | solution.py:147
  84.4 2.4 %shard_map.196.refs_2_ = bf16[256,128]{1,0:T(8,128)(2,1)S(1)} custom-call(f32[256,128]{1,0:T(8,128)S(1)} %get-tuple-element.43.refs_0_, bf16[1024,256]{1,0:T(8,128)(2,1)S(1)} %pad_maximum_fusion.refs_1_.refs_5_, bf16[512,256]{1,0:T(8,128)(2,1)S(1)} %pad_maximum_fusion.1.refs_2_.refs_4_, bf16[512,256]{1,0:T(8,128)(2,1)S(1)} %collective-permute-done.8.refs_3_, ...), custom_call_target="tpu_custom_call" | custom-call | tf_op jit(solution)/shard_map/pallas_call | solution.py:263
  86.8 4.2 %all-to-all-done.2.refs_1_ = bf16[16,8,1152]{2,1,0:T(8,128)(2,1)S(1)} async-done(((bf16[16,8,1152]{2,1,0:T(8,128)(2,1)}), bf16[16,8,1152]{2,1,0:T(8,128)(2,1)S(1)}, u32[]{:S(2)}, u32[]{:S(2)}) %all-to-all-start.2) | async-done | bytes 294944 | tf_op jit(solution)/shard_map/all_to_all | solution.py:147
  91.0 4.2 %shard_map.197 = bf16[256,512]{1,0:T(8,128)(2,1)S(1)} custom-call(s32[16]{0:T(128)S(1)} %fusion.5.refs_0_, bf16[16,8,1152]{2,1,0:T(8,128)(2,1)S(1)} %all-to-all-done.2.refs_1_, bf16[256,128]{1,0:T(8,128)(2,1)S(1)} %shard_map.196.refs_2_, bf16[256,128]{1,0:T(8,128)(2,1)S(1)} %get-tuple-element.44.refs_3_, ...), custom_call_target="tpu_custom_call" | custom-call | tf_op jit(solution)/shard_map/pallas_call | solution.py:263
  95.2 12.5 %all_to_all.21.refs_0_.refs_5_ = bf16[8,32,512]{2,1,0:T(8,128)(2,1)S(1)} all-to-all(bf16[8,32,512]{2,1,0:T(8,128)(2,1)S(1)} %bitcast.15), channel_id=1, replica_groups=mesh['row'=8,'col'=16] {'row'}, dimensions={0} | all-to-all | bytes 524288 | tf_op jit(solution)/shard_map/all_to_all | solution.py:147
  107.8 8.5 %shard_map.198 = (bf16[512,512]{1,0:T(8,128)(2,1)S(1)}, bf16[512,256]{1,0:T(8,128)(2,1)}, bf16[96,512]{1,0:T(8,128)(2,1)S(1)}, bf16[96,512]{1,0:T(8,128)(2,1)S(1...) custom-call(bf16[8,32,512]{2,1,0:T(8,128)(2,1)S(1)} %all_to_all.21.refs_0_.refs_5_, ...), custom_call_target="tpu_custom_call" | custom-call | tf_op jit(solution)/shard_map/pallas_call | solution.py:263
  116.3 2.5 %collective-permute-start.18 = (bf16[96,512]{1,0:T(8,128)(2,1)S(1)}, bf16[96,512]{1,0:T(8,128)(2,1)S(1)}, u32[]{:S(2)}, u32[]{:S(2)}) collective-permute-start(bf16[96,512]{1,0:T(8,128)(2,1)S(1)} %get-tuple-element.49), channel_id=1, source_target_pairs={{0,16},{16,32},{32,48},{48,64},{64,80},{80,96},{96,112},{1,17},{17... | collective-permute-start | bytes 294920 | tf_op jit(solution)/shard_map/ppermute | solution.py:118
  118.8 3.6 %collective-permute-start.19 = (bf16[96,512]{1,0:T(8,128)(2,1)S(1)}, bf16[96,512]{1,0:T(8,128)(2,1)S(1)}, u32[]{:S(2)}, u32[]{:S(2)}) collective-permute-start(bf16[96,512]{1,0:T(8,128)(2,1)S(1)} %get-tuple-element.50), channel_id=1, source_target_pairs={{16,0},{32,16},{48,32},{64,48},{80,64},{96,80},{112,96},{17,1},{33... | collective-permute-start | bytes 294920 | tf_op jit(solution)/shard_map/ppermute | solution.py:118
  122.4 4.3 %shard_map.199.refs_12_ = f32[512,256]{1,0:T(8,128)S(1)} custom-call(bf16[512,256]{1,0:T(8,128)(2,1)} %get-tuple-element.47.refs_8_.refs_0_, bf16[896,256]{1,0:T(8,128)(2,1)} %get-tuple-element.51.refs_1_.refs_0_, bf16[512,512]{1,0:T(8,128)(2,1)S(1)} %get-tuple-element.52.refs_2_, bf16[896,256]{1,0:T(8,128)(2,1)} %get-tuple-element.53.refs_3_.refs_1_, ...), custom_call_target="tpu_custom_call" | custom-call | tf_op jit(solution)/shard_map/pallas_call | solution.py:263
  126.9 1.9 %collective-permute-start.20 = (bf16[80,512]{1,0:T(8,128)(2,1)S(1)}, bf16[80,512]{1,0:T(8,128)(2,1)S(1)}, u32[]{:S(2)}, u32[]{:S(2)}) collective-permute-start(bf16[80,512]{1,0:T(8,128)(2,1)S(1)} %get-tuple-element.64), channel_id=1, source_target_pairs={{0,1},{1,2},{2,3},{3,4},{4,5},{5,6},{6,7},{7,8},{8,9},{9,10},{10,1... | collective-permute-start | bytes 245768 | tf_op jit(solution)/shard_map/ppermute | solution.py:118
  128.9 6.0 %collective-permute-start.21 = (bf16[80,512]{1,0:T(8,128)(2,1)S(1)}, bf16[80,512]{1,0:T(8,128)(2,1)S(1)}, u32[]{:S(2)}, u32[]{:S(2)}) collective-permute-start(bf16[80,512]{1,0:T(8,128)(2,1)S(1)} %get-tuple-element.65), channel_id=1, source_target_pairs={{1,0},{2,1},{3,2},{4,3},{5,4},{6,5},{7,6},{8,7},{9,8},{10,9},{11,1... | collective-permute-start | bytes 245768 | tf_op jit(solution)/shard_map/ppermute | solution.py:118
  135.6 5.7 %shard_map.201 = (f32[512,256]{1,0:T(8,128)S(1)}, bf16[32,1024]{1,0:T(8,128)(2,1)}) custom-call(bf16[512,256]{1,0:T(8,128)(2,1)} %get-tuple-element.60.refs_9_.refs_0_, bf16[896,256]{1,0:T(8,128)(2,1)} %get-tuple-element.61.refs_1_.refs_2_, bf16[512,512]{1,0:T(8,128)(2,1)S(1)} %get-tuple-element.52.refs_2_, bf16[896,256]{1,0:T(8,128)(2,1)} %get-tuple-element.62.refs_3_, ...), custom_call_target="tpu_custom_call" | custom-call | tf_op jit(solution)/shard_map/pallas_call | solution.py:263
  141.3 5.9 %shard_map.202 = bf16[512,256]{1,0:T(8,128)(2,1)} custom-call(bf16[896,256]{1,0:T(8,128)(2,1)} %get-tuple-element.51.refs_1_.refs_0_, bf16[896,256]{1,0:T(8,128)(2,1)} %get-tuple-element.53.refs_3_.refs_1_, bf16[896,256]{1,0:T(8,128)(2,1)} %get-tuple-element.61.refs_1_.refs_2_, bf16[896,256]{1,0:T(8,128)(2,1)} %get-tuple-element.62.refs_3_, ...), custom_call_target="tpu_custom_call" | custom-call | tf_op jit(solution)/shard_map/pallas_call | solution.py:263
  (57 shorter events, 10.9 us)
Async XLA Ops:
  0.6 10.0 %copy-start.4 = (s32[384]{0:T(512)S(1)}, s32[384]{0:T(512)}, u32[]{:S(2)}) copy-start(s32[384]{0:T(512)} %constant.117.clone) | copy-start | bytes 4612
  0.6 10.0 %copy-start.5 = (s32[384]{0:T(512)S(1)}, s32[384]{0:T(512)}, u32[]{:S(2)}) copy-start(s32[384]{0:T(512)} %constant.116.clone) | copy-start | bytes 4612
  0.7 11.2 %copy-start = (bf16[32,96]{1,0:T(8,128)(2,1)S(1)}, bf16[32,96]{1,0:T(8,128)(2,1)}, u32[]{:S(2)}) copy-start(bf16[32,96]{1,0:T(8,128)(2,1)} %constant.114.clone.refs_0_) | copy-start | bytes 18436
  0.7 19.4 %copy-start.3 = (bf16[384,128]{1,0:T(8,128)(2,1)S(1)}, bf16[384,128]{1,0:T(8,128)(2,1)}, u32[]{:S(2)}) copy-start(bf16[384,128]{1,0:T(8,128)(2,1)} %constant.158) | copy-start | bytes 294916
  1.5 9.2 %collective-permute-start = (bf16[96,256]{1,0:T(8,128)(2,1)S(1)}, bf16[96,256]{1,0:T(8,128)(2,1)S(1)}, u32[]{:S(2)}, u32[]{:S(2)}) collective-permute-start(bf16[96,256]{1,0:T(8,128)(2,1)S(1)} %bitcast.22), channel_id=1, source_target_pairs={{0,16},{16,32},{32,48},{48,64},{64,80},{80,96},{96,112},{1,17},{17... | collective-permute-start | bytes 147464 | tf_op jit(solution)/shard_map/ppermute | solution.py:118
  5.0 6.9 %collective-permute-start.1 = (bf16[96,256]{1,0:T(8,128)(2,1)S(1)}, bf16[96,256]{1,0:T(8,128)(2,1)S(1)}, u32[]{:S(2)}, u32[]{:S(2)}) collective-permute-start(bf16[96,256]{1,0:T(8,128)(2,1)S(1)} %bitcast.21), channel_id=1, source_target_pairs={{16,0},{32,16},{48,32},{64,48},{80,64},{96,80},{112,96},{17,1},{33... | collective-permute-start | bytes 147464 | tf_op jit(solution)/shard_map/ppermute | solution.py:118
  12.1 8.8 %collective-permute-start.2 = (bf16[80,256]{1,0:T(8,128)(2,1)S(1)}, bf16[80,256]{1,0:T(8,128)(2,1)S(1)}, u32[]{:S(2)}, u32[]{:S(2)}) collective-permute-start(bf16[80,256]{1,0:T(8,128)(2,1)S(1)} %get-tuple-element.37), channel_id=1, source_target_pairs={{0,1},{1,2},{2,3},{3,4},{4,5},{5,6},{6,7},{7,8},{8,9},{9,10},{10,1... | collective-permute-start | bytes 122888 | tf_op jit(solution)/shard_map/ppermute | solution.py:118
  14.0 7.7 %collective-permute-start.3 = (bf16[80,256]{1,0:T(8,128)(2,1)S(1)}, bf16[80,256]{1,0:T(8,128)(2,1)S(1)}, u32[]{:S(2)}, u32[]{:S(2)}) collective-permute-start(bf16[80,256]{1,0:T(8,128)(2,1)S(1)} %get-tuple-element.38), channel_id=1, source_target_pairs={{1,0},{2,1},{3,2},{4,3},{5,4},{6,5},{7,6},{8,7},{9,8},{10,9},{11,1... | collective-permute-start | bytes 122888 | tf_op jit(solution)/shard_map/ppermute | solution.py:118
  31.4 28.3 %copy-start.2 = (bf16[4,8,1024]{2,1,0:T(8,128)(2,1)S(1)}, bf16[4,8,1024]{2,1,0:T(8,128)(2,1)}, u32[]{:S(2)}) copy-start(bf16[4,8,1024]{2,1,0:T(8,128)(2,1)} %param.25) | copy-start | bytes 196612
  44.2 7.9 %collective-permute-start.7 = (bf16[256,256]{1,0:T(8,128)(2,1)S(1)}, bf16[256,256]{1,0:T(8,128)(2,1)S(1)}, u32[]{:S(2)}, u32[]{:S(2)}) collective-permute-start(bf16[256,256]{1,0:T(8,128)(2,1)S(1)} %get-tuple-element.71), channel_id=1, source_target_pairs={{0,8},{1,9},{2,10},{3,11},{4,12},{5,13},{6,14},{7,15},{8,0},{9,1},... | collective-permute-start | bytes 393224 | tf_op jit(solution)/shard_map/ppermute | solution.py:111
  47.2 6.9 %collective-permute-start.6 = (bf16[256,256]{1,0:T(8,128)(2,1)S(1)}, bf16[256,256]{1,0:T(8,128)(2,1)S(1)}, u32[]{:S(2)}, u32[]{:S(2)}) collective-permute-start(bf16[256,256]{1,0:T(8,128)(2,1)S(1)} %get-tuple-element.71), channel_id=1, source_target_pairs={{0,12},{1,13},{2,14},{3,15},{4,0},{5,1},{6,2},{7,3},{8,4},{9,5},{1... | collective-permute-start | bytes 393224 | tf_op jit(solution)/shard_map/ppermute | solution.py:111
  48.2 6.3 %collective-permute-start.5 = (bf16[256,256]{1,0:T(8,128)(2,1)S(1)}, bf16[256,256]{1,0:T(8,128)(2,1)S(1)}, u32[]{:S(2)}, u32[]{:S(2)}) collective-permute-start(bf16[256,256]{1,0:T(8,128)(2,1)S(1)} %get-tuple-element.71), channel_id=1, source_target_pairs={{0,4},{1,5},{2,6},{3,7},{4,8},{5,9},{6,10},{7,11},{8,12},{9,13},{1... | collective-permute-start | bytes 393224 | tf_op jit(solution)/shard_map/ppermute | solution.py:111
  49.3 6.5 %collective-permute-start.4 = (bf16[256,256]{1,0:T(8,128)(2,1)S(1)}, bf16[256,256]{1,0:T(8,128)(2,1)S(1)}, u32[]{:S(2)}, u32[]{:S(2)}) collective-permute-start(bf16[256,256]{1,0:T(8,128)(2,1)S(1)} %get-tuple-element.72), channel_id=1, source_target_pairs={{0,2},{1,3},{2,0},{3,1},{4,6},{5,7},{6,4},{7,5},{8,10},{9,11},{10,... | collective-permute-start | bytes 393224 | tf_op jit(solution)/shard_map/ppermute | solution.py:111
  54.6 16.8 %collective-permute-start.15 = (bf16[1024,256]{1,0:T(8,128)(2,1)S(1)}, bf16[1024,256]{1,0:T(8,128)(2,1)}, u32[]{:S(2)}, u32[]{:S(2)}) collective-permute-start(bf16[1024,256]{1,0:T(8,128)(2,1)S(1)} %pad_maximum_fusion.refs_1_.refs_5_), channel_id=1, source_target_pairs={{0,2},{1,3},{2,0},{3,1},{4,6},{5,7},{6,4},{7,5},{8,10},{9,11},{10,... | collective-permute-start | bytes 1572872 | tf_op jit(solution)/shard_map/ppermute | solution.py:111
  55.8 9.4 %collective-permute-start.8 = (bf16[512,256]{1,0:T(8,128)(2,1)S(1)}, bf16[512,256]{1,0:T(8,128)(2,1)S(1)}, u32[]{:S(2)}, u32[]{:S(2)}) collective-permute-start(bf16[512,256]{1,0:T(8,128)(2,1)S(1)} %pad_maximum_fusion.1.refs_2_.refs_4_), channel_id=1, source_target_pairs={{0,4},{1,5},{2,6},{3,7},{4,8},{5,9},{6,10},{7,11},{8,12},{9,13},{1... | collective-permute-start | bytes 786440 | tf_op jit(solution)/shard_map/ppermute | solution.py:111
  57.5 9.2 %collective-permute-start.9 = (bf16[512,256]{1,0:T(8,128)(2,1)S(1)}, bf16[512,256]{1,0:T(8,128)(2,1)S(1)}, u32[]{:S(2)}, u32[]{:S(2)}) collective-permute-start(bf16[512,256]{1,0:T(8,128)(2,1)S(1)} %pad_maximum_fusion.1.refs_2_.refs_4_), channel_id=1, source_target_pairs={{0,12},{1,13},{2,14},{3,15},{4,0},{5,1},{6,2},{7,3},{8,4},{9,5},{1... | collective-permute-start | bytes 786440 | tf_op jit(solution)/shard_map/ppermute | solution.py:111
  57.9 13.0 %collective-permute-start.10 = (bf16[512,256]{1,0:T(8,128)(2,1)S(1)}, bf16[512,256]{1,0:T(8,128)(2,1)S(1)}, u32[]{:S(2)}, u32[]{:S(2)}) collective-permute-start(bf16[512,256]{1,0:T(8,128)(2,1)S(1)} %pad_maximum_fusion.1.refs_2_.refs_4_), channel_id=1, source_target_pairs={{0,8},{1,9},{2,10},{3,11},{4,12},{5,13},{6,14},{7,15},{8,0},{9,1},... | collective-permute-start | bytes 786440 | tf_op jit(solution)/shard_map/ppermute | solution.py:111
  60.5 14.8 %all-to-all-start.1 = ((bf16[8,32,1024]{2,1,0:T(8,128)(2,1)}), bf16[8,32,1024]{2,1,0:T(8,128)(2,1)S(1)}, u32[]{:S(2)}, u32[]{:S(2)}) async-start(bf16[8,32,1024]{2,1,0:T(8,128)(2,1)} %broadcast_in_dim.7), calls=%async_computation.1 | async-start | bytes 1048576 | tf_op jit(solution)/shard_map/all_to_all | solution.py:147
  65.2 18.5 %copy-start.1 = (s32[4]{0:T(128)S(1)}, s32[4]{0:T(128)}, u32[]{:S(2)}) copy-start(s32[4]{0:T(128)} %constant.119.clone) | copy-start | bytes 52
  65.2 5.7 %collective-permute-start.11 = (bf16[512,256]{1,0:T(8,128)(2,1)S(1)}, bf16[512,256]{1,0:T(8,128)(2,1)S(1)}, u32[]{:S(2)}, u32[]{:S(2)}) collective-permute-start(bf16[512,256]{1,0:T(8,128)(2,1)S(1)} %pad_maximum_fusion.1.refs_2_.refs_4_), channel_id=1, source_target_pairs={{0,1},{1,0},{2,3},{3,2},{4,5},{5,4},{6,7},{7,6},{8,9},{9,8},{10,11... | collective-permute-start | bytes 786440 | tf_op jit(solution)/shard_map/ppermute | solution.py:111
  65.2 10.1 %collective-permute-start.12 = (bf16[512,256]{1,0:T(8,128)(2,1)S(1)}, bf16[512,256]{1,0:T(8,128)(2,1)S(1)}, u32[]{:S(2)}, u32[]{:S(2)}) collective-permute-start(bf16[512,256]{1,0:T(8,128)(2,1)S(1)} %collective-permute-done.8.refs_3_), channel_id=1, source_target_pairs={{0,1},{1,0},{2,3},{3,2},{4,5},{5,4},{6,7},{7,6},{8,9},{9,8},{10,11... | collective-permute-start | bytes 786440 | tf_op jit(solution)/shard_map/ppermute | solution.py:111
  66.7 8.6 %collective-permute-start.13 = (bf16[512,256]{1,0:T(8,128)(2,1)S(1)}, bf16[512,256]{1,0:T(8,128)(2,1)S(1)}, u32[]{:S(2)}, u32[]{:S(2)}) collective-permute-start(bf16[512,256]{1,0:T(8,128)(2,1)S(1)} %collective-permute-done.9.refs_4_), channel_id=1, source_target_pairs={{0,1},{1,0},{2,3},{3,2},{4,5},{5,4},{6,7},{7,6},{8,9},{9,8},{10,11... | collective-permute-start | bytes 786440 | tf_op jit(solution)/shard_map/ppermute | solution.py:111
  70.9 4.5 %collective-permute-start.14 = (bf16[512,256]{1,0:T(8,128)(2,1)S(1)}, bf16[512,256]{1,0:T(8,128)(2,1)S(1)}, u32[]{:S(2)}, u32[]{:S(2)}) collective-permute-start(bf16[512,256]{1,0:T(8,128)(2,1)S(1)} %collective-permute-done.10.refs_5_), channel_id=1, source_target_pairs={{0,1},{1,0},{2,3},{3,2},{4,5},{5,4},{6,7},{7,6},{8,9},{9,8},{10,11... | collective-permute-start | bytes 786440 | tf_op jit(solution)/shard_map/ppermute | solution.py:111
  70.9 15.9 %collective-permute-start.16 = (bf16[1024,256]{1,0:T(8,128)(2,1)S(1)}, bf16[1024,256]{1,0:T(8,128)(2,1)}, u32[]{:S(2)}, u32[]{:S(2)}) collective-permute-start(bf16[1024,256]{1,0:T(8,128)(2,1)S(1)} %pad_maximum_fusion.refs_1_.refs_5_), channel_id=1, source_target_pairs={{0,1},{1,0},{2,3},{3,2},{4,5},{5,4},{6,7},{7,6},{8,9},{9,8},{10,11... | collective-permute-start | bytes 1572872 | tf_op jit(solution)/shard_map/ppermute | solution.py:111
  71.4 19.6 %collective-permute-start.17 = (bf16[1024,256]{1,0:T(8,128)(2,1)}, bf16[1024,256]{1,0:T(8,128)(2,1)}, u32[]{:S(2)}, u32[]{:S(2)}) collective-permute-start(bf16[1024,256]{1,0:T(8,128)(2,1)} %collective-permute-done.15.refs_6_), channel_id=1, source_target_pairs={{0,1},{1,0},{2,3},{3,2},{4,5},{5,4},{6,7},{7,6},{8,9},{9,8},{10,11... | collective-permute-start | bytes 1572872 | tf_op jit(solution)/shard_map/ppermute | solution.py:111
  78.4 12.6 %all-to-all-start.2 = ((bf16[16,8,1152]{2,1,0:T(8,128)(2,1)}), bf16[16,8,1152]{2,1,0:T(8,128)(2,1)S(1)}, u32[]{:S(2)}, u32[]{:S(2)}) async-start(bf16[16,8,1152]{2,1,0:T(8,128)(2,1)} %get-tuple-element.42), calls=%async_computation.2 | async-start | bytes 589824 | tf_op jit(solution)/shard_map/all_to_all | solution.py:147
  116.3 10.4 %collective-permute-start.18 = (bf16[96,512]{1,0:T(8,128)(2,1)S(1)}, bf16[96,512]{1,0:T(8,128)(2,1)S(1)}, u32[]{:S(2)}, u32[]{:S(2)}) collective-permute-start(bf16[96,512]{1,0:T(8,128)(2,1)S(1)} %get-tuple-element.49), channel_id=1, source_target_pairs={{0,16},{16,32},{32,48},{48,64},{64,80},{80,96},{96,112},{1,17},{17... | collective-permute-start | bytes 294920 | tf_op jit(solution)/shard_map/ppermute | solution.py:118
  118.8 7.9 %collective-permute-start.19 = (bf16[96,512]{1,0:T(8,128)(2,1)S(1)}, bf16[96,512]{1,0:T(8,128)(2,1)S(1)}, u32[]{:S(2)}, u32[]{:S(2)}) collective-permute-start(bf16[96,512]{1,0:T(8,128)(2,1)S(1)} %get-tuple-element.50), channel_id=1, source_target_pairs={{16,0},{32,16},{48,32},{64,48},{80,64},{96,80},{112,96},{17,1},{33... | collective-permute-start | bytes 294920 | tf_op jit(solution)/shard_map/ppermute | solution.py:118
  126.9 14.3 %collective-permute-start.20 = (bf16[80,512]{1,0:T(8,128)(2,1)S(1)}, bf16[80,512]{1,0:T(8,128)(2,1)S(1)}, u32[]{:S(2)}, u32[]{:S(2)}) collective-permute-start(bf16[80,512]{1,0:T(8,128)(2,1)S(1)} %get-tuple-element.64), channel_id=1, source_target_pairs={{0,1},{1,2},{2,3},{3,4},{4,5},{5,6},{6,7},{7,8},{8,9},{9,10},{10,1... | collective-permute-start | bytes 245768 | tf_op jit(solution)/shard_map/ppermute | solution.py:118
  128.9 12.4 %collective-permute-start.21 = (bf16[80,512]{1,0:T(8,128)(2,1)S(1)}, bf16[80,512]{1,0:T(8,128)(2,1)S(1)}, u32[]{:S(2)}, u32[]{:S(2)}) collective-permute-start(bf16[80,512]{1,0:T(8,128)(2,1)S(1)} %get-tuple-element.65), channel_id=1, source_target_pairs={{1,0},{2,1},{3,2},{4,3},{5,4},{6,5},{7,6},{8,7},{9,8},{10,9},{11,1... | collective-permute-start | bytes 245768 | tf_op jit(solution)/shard_map/ppermute | solution.py:118
where the time goes:
time: 148 us; the launch traced here: 147 us
  starting transfers between devices  49 us (33%)
  Pallas kernels  44.1 us (30%)
  blocking collectives  25.3 us (17%)
  waiting for transfers between devices  20.5 us (14%)
  local copies, waits for them, and re-layouts  3.43 us (2%)
  matrix products  2.34 us (2%)
  other arithmetic  1.52 us (1%)
    pallas_call x10, Pallas kernels, call(): pl.pallas_call(body, out_shape=[pltpu.HBM(*out) if i in out_manual else j...  44.1 us
    all_to_all x2, blocking collectives, all_to_all(): return lax.all_to_all(array, axis, split_axis=0, concat_axis=0, tiled=True)  25.3 us
    ppermute x4, starting transfers between devices, neighbours(): lax.ppermute(to_previous, axis, down)  18.1 us
    ppermute x14, starting transfers between devices, shifted(): return lax.ppermute(array, axis, [(i, move(i)) for i in range(count)])  11.2 us
    ppermute x14, waiting for transfers between devices, shifted(): return lax.ppermute(array, axis, [(i, move(i)) for i in range(count)])  10.6 us
    all_to_all x2, starting transfers between devices, all_to_all(): return lax.all_to_all(array, axis, split_axis=0, concat_axis=0, tiled=True)  9.92 us
    ppermute x4, starting transfers between devices, neighbours(): lax.ppermute(to_next, axis, up)  9.76 us
    all_to_all x2, waiting for transfers between devices, all_to_all(): return lax.all_to_all(array, axis, split_axis=0, concat_axis=0, tiled=True)  7.89 us
  transfers between devices with their start and end apart: 24, of which 10 were waited for; matrix products, arithmetic and copies ran while one was open for 4% of the time, Pallas kernels for 11%

commit v1 on v0

--- a/solution.py
+++ b/solution.py
@@ -408,6 +408,7 @@
         m2 += dot(m1[part * tokens : (part + 1) * tokens], two_ref[part * C1 : (part + 1) * C1])
     m2 = m2.astype(bf16)
     m2_out[...] = m2
+    m2_out.send()
     m2f = m2.astype(f32)
     mn = (m2f * rms_stat(m2f)).astype(bf16)
     dim = C2 // GHEADS
@@ -525,6 +526,7 @@
     du1 = dot_last(jnp.concatenate(dm1, 0), one_ref[...]).astype(bf16)
     dy = jnp.concatenate([du1[:, part * C0 : (part + 1) * C0] for part in range(4)], 0)
     dy_out[...] = dy
+    dy_out.send()
     da0 = dot_last(dy, w_out_ref[...]).astype(bf16).astype(f32)
     lane = lax.broadcasted_iota(jnp.int32, (1, LANES), 1)
     is_lse = (lane == LSE_LANE) | (lane == LSE_LANE + 1)
@@ -587,16 +589,16 @@
 
 
 def na_beside_kernel(
+    hot_ref,
+    q_halo_ref,
     k_one,
     v_one,
     k_two,
     v_two,
-    hot_ref,
     before_ref,
     after_ref,
     left_ref,
     right_ref,
-    q_halo_ref,
     w_ref,
     x_ref,
     dxn_one,
@@ -789,16 +791,16 @@
         na_beside_kernel,
         [((own, C0), bf16)],
         (
+            hot,
+            q0_halo,
             Rows(k_one, own),
             Rows(v_one, own),
             Rows(k_two, own),
             Rows(v_two, own),
-            hot,
             before,
             after,
             left,
             right,
-            q0_halo,
             na_qkv,
             xp,
             dxn_one,
@@ -806,7 +808,7 @@
             dy0,
             perm_back,
         ),
-        manual=(0, 1, 2, 3, 4, 9, 10, 11, 14, 15),
+        manual=(0, 1, 2, 3, 4, 5, 10, 11, 14, 15),
         scratch=(pltpu.VMEM((padded, WIDE), bf16),),
     )[0]
     return (

time: 148 us -> 147 us (level)
  no operation moved by 1% of the time
where the time goes in v1:
time: 147 us
  starting transfers between devices  49 us (33%)
  Pallas kernels  43.5 us (30%)
  blocking collectives  25.3 us (17%)
  waiting for transfers between devices  20.5 us (14%)
  local copies, waits for them, and re-layouts  3.43 us (2%)
  matrix products  2.34 us (2%)
  other arithmetic  1.52 us (1%)
    pallas_call x10, Pallas kernels, call(): pl.pallas_call(body, out_shape=[pltpu.HBM(*out) if i in out_manual else j...  43.5 us
    all_to_all x2, blocking collectives, all_to_all(): return lax.all_to_all(array, axis, split_axis=0, concat_axis=0, tiled=True)  25.3 us
    ppermute x4, starting transfers between devices, neighbours(): lax.ppermute(to_previous, axis, down)  18.1 us
    ppermute x14, starting transfers between devices, shifted(): return lax.ppermute(array, axis, [(i, move(i)) for i in range(count)])  11.2 us
    ppermute x14, waiting for transfers between devices, shifted(): return lax.ppermute(array, axis, [(i, move(i)) for i in range(count)])  10.6 us
    all_to_all x2, starting transfers between devices, all_to_all(): return lax.all_to_all(array, axis, split_axis=0, concat_axis=0, tiled=True)  9.93 us
    ppermute x4, starting transfers between devices, neighbours(): lax.ppermute(to_next, axis, up)  9.76 us
    all_to_all x2, waiting for transfers between devices, all_to_all(): return lax.all_to_all(array, axis, split_axis=0, concat_axis=0, tiled=True)  7.88 us
  transfers between devices with their start and end apart: 24, of which 10 were waited for; matrix products, arithmetic and copies ran while one was open for 4% of the time, Pallas kernels for 11%

profile of v1, /device:TPU:34, one launch (start us, length us, event | category | flops | bytes accessed | tf_op | source)
XLA Modules:
  0.0 146.7 jit_solution(14130126285263797379)
XLA Ops:
  1.5 3.4 %collective-permute-start = (bf16[96,256]{1,0:T(8,128)(2,1)S(1)}, bf16[96,256]{1,0:T(8,128)(2,1)S(1)}, u32[]{:S(2)}, u32[]{:S(2)}) collective-permute-start(bf16[96,256]{1,0:T(8,128)(2,1)S(1)} %bitcast.22), channel_id=1, source_target_pairs={{0,16},{16,32},{32,48},{48,64},{64,80},{80,96},{96,112},{1,17},{17... | collective-permute-start | bytes 147464 | tf_op jit(solution)/shard_map/ppermute | solution.py:118
  5.0 2.4 %collective-permute-start.1 = (bf16[96,256]{1,0:T(8,128)(2,1)S(1)}, bf16[96,256]{1,0:T(8,128)(2,1)S(1)}, u32[]{:S(2)}, u32[]{:S(2)}) collective-permute-start(bf16[96,256]{1,0:T(8,128)(2,1)S(1)} %bitcast.21), channel_id=1, source_target_pairs={{16,0},{32,16},{48,32},{64,48},{80,64},{96,80},{112,96},{17,1},{33... | collective-permute-start | bytes 147464 | tf_op jit(solution)/shard_map/ppermute | solution.py:118
  8.3 2.3 %convolution_convert_fusion.refs_14_ = bf16[32,1024]{1,0:T(8,128)(2,1)S(1)} fusion(bf16[1024,1024]{1,0:T(8,128)(2,1)} %refs_6_.3, bf16[4,8,1024]{2,1,0:T(8,128)(2,1)} %param.25), kind=kOutput, calls=%fused_computation.1 | convolution fusion | flops 67141632 | bytes 2228224 | tf_op jit(solution)/shard_map/dot_general | solution.py:37
  10.8 1.1 collective-permute-done.1.refs_2_.refs_4_
  12.1 1.9 %collective-permute-start.2 = (bf16[80,256]{1,0:T(8,128)(2,1)S(1)}, bf16[80,256]{1,0:T(8,128)(2,1)S(1)}, u32[]{:S(2)}, u32[]{:S(2)}) collective-permute-start(bf16[80,256]{1,0:T(8,128)(2,1)S(1)} %get-tuple-element.37), channel_id=1, source_target_pairs={{0,1},{1,2},{2,3},{3,4},{4,5},{5,6},{6,7},{7,8},{8,9},{9,10},{10,1... | collective-permute-start | bytes 122888 | tf_op jit(solution)/shard_map/ppermute | solution.py:118
  14.0 6.0 %collective-permute-start.3 = (bf16[80,256]{1,0:T(8,128)(2,1)S(1)}, bf16[80,256]{1,0:T(8,128)(2,1)S(1)}, u32[]{:S(2)}, u32[]{:S(2)}) collective-permute-start(bf16[80,256]{1,0:T(8,128)(2,1)S(1)} %get-tuple-element.38), channel_id=1, source_target_pairs={{1,0},{2,1},{3,2},{4,3},{5,4},{6,5},{7,6},{8,7},{9,8},{10,9},{11,1... | collective-permute-start | bytes 122888 | tf_op jit(solution)/shard_map/ppermute | solution.py:118
  21.7 9.5 %shard_map.194 = (bf16[8,32,512]{2,1,0:T(8,128)(2,1)S(1)}, bf16[32,1024]{1,0:T(8,128)(2,1)}, bf16[512,256]{1,0:T(8,128)(2,1)}, bf16[512,256]{1,0:T(8,128)(2,1)},...) custom-call(bf16[512,256]{1,0:T(8,128)(2,1)} %bitcast.17, ...), custom_call_target="tpu_custom_call" | custom-call | tf_op jit(solution)/shard_map/pallas_call | solution.py:263
  31.2 12.8 %all_to_all.20 = bf16[8,32,512]{2,1,0:T(8,128)(2,1)S(1)} all-to-all(bf16[8,32,512]{2,1,0:T(8,128)(2,1)S(1)} %get-tuple-element.39), channel_id=1, replica_groups=mesh['row'=8,'col'=16] {'row'}, dimensions={0} | all-to-all | bytes 524288 | tf_op jit(solution)/shard_map/all_to_all | solution.py:147
  44.0 3.1 %collective-permute-start.7 = (bf16[256,256]{1,0:T(8,128)(2,1)S(1)}, bf16[256,256]{1,0:T(8,128)(2,1)S(1)}, u32[]{:S(2)}, u32[]{:S(2)}) collective-permute-start(bf16[256,256]{1,0:T(8,128)(2,1)S(1)} %get-tuple-element.71), channel_id=1, source_target_pairs={{0,8},{1,9},{2,10},{3,11},{4,12},{5,13},{6,14},{7,15},{8,0},{9,1},... | collective-permute-start | bytes 393224 | tf_op jit(solution)/shard_map/ppermute | solution.py:111
  48.1 1.0 collective-permute-start.5
  49.5 2.4 %collective-permute-done.7 = bf16[256,256]{1,0:T(8,128)(2,1)S(1)} collective-permute-done((bf16[256,256]{1,0:T(8,128)(2,1)S(1)}, bf16[256,256]{1,0:T(8,128)(2,1)S(1)}, u32[]{:S(2)}, u32[]{:S(2)}) %collective-permute-start.7) | collective-permute-done | bytes 131104 | tf_op jit(solution)/shard_map/ppermute | solution.py:111
  51.9 2.0 %collective-permute-done.6 = bf16[256,256]{1,0:T(8,128)(2,1)S(1)} collective-permute-done((bf16[256,256]{1,0:T(8,128)(2,1)S(1)}, bf16[256,256]{1,0:T(8,128)(2,1)S(1)}, u32[]{:S(2)}, u32[]{:S(2)}) %collective-permute-start.6) | collective-permute-done | bytes 131104 | tf_op jit(solution)/shard_map/ppermute | solution.py:111
  55.6 1.7 %collective-permute-start.8 = (bf16[512,256]{1,0:T(8,128)(2,1)S(1)}, bf16[512,256]{1,0:T(8,128)(2,1)S(1)}, u32[]{:S(2)}, u32[]{:S(2)}) collective-permute-start(bf16[512,256]{1,0:T(8,128)(2,1)S(1)} %pad_maximum_fusion.1.refs_2_.refs_4_), channel_id=1, source_target_pairs={{0,4},{1,5},{2,6},{3,7},{4,8},{5,9},{6,10},{7,11},{8,12},{9,13},{1... | collective-permute-start | bytes 786440 | tf_op jit(solution)/shard_map/ppermute | solution.py:111
  57.7 1.8 %collective-permute-start.10 = (bf16[512,256]{1,0:T(8,128)(2,1)S(1)}, bf16[512,256]{1,0:T(8,128)(2,1)S(1)}, u32[]{:S(2)}, u32[]{:S(2)}) collective-permute-start(bf16[512,256]{1,0:T(8,128)(2,1)S(1)} %pad_maximum_fusion.1.refs_2_.refs_4_), channel_id=1, source_target_pairs={{0,8},{1,9},{2,10},{3,11},{4,12},{5,13},{6,14},{7,15},{8,0},{9,1},... | collective-permute-start | bytes 786440 | tf_op jit(solution)/shard_map/ppermute | solution.py:111
  60.3 4.7 %all-to-all-start.1 = ((bf16[8,32,1024]{2,1,0:T(8,128)(2,1)}), bf16[8,32,1024]{2,1,0:T(8,128)(2,1)S(1)}, u32[]{:S(2)}, u32[]{:S(2)}) async-start(bf16[8,32,1024]{2,1,0:T(8,128)(2,1)} %broadcast_in_dim.7), calls=%async_computation.1 | async-start | bytes 1048576 | tf_op jit(solution)/shard_map/all_to_all | solution.py:147
  65.5 1.0 collective-permute-done.9.refs_4_
  66.6 4.2 %collective-permute-done.10.refs_5_ = bf16[512,256]{1,0:T(8,128)(2,1)S(1)} collective-permute-done((bf16[512,256]{1,0:T(8,128)(2,1)S(1)}, bf16[512,256]{1,0:T(8,128)(2,1)S(1)}, u32[]{:S(2)}, u32[]{:S(2)}) %collective-permute-start.10) | collective-permute-done | bytes 262176 | tf_op jit(solution)/shard_map/ppermute | solution.py:111
  71.5 3.7 %all-to-all-done.1 = bf16[8,32,1024]{2,1,0:T(8,128)(2,1)S(1)} async-done(((bf16[8,32,1024]{2,1,0:T(8,128)(2,1)}), bf16[8,32,1024]{2,1,0:T(8,128)(2,1)S(1)}, u32[]{:S(2)}, u32[]{:S(2)}) %all-to-all-start.1) | async-done | bytes 524320 | tf_op jit(solution)/shard_map/all_to_all | solution.py:147
  75.2 3.1 %shard_map.195 = (bf16[256,128]{1,0:T(8,128)(2,1)S(1)}, f32[256,128]{1,0:T(8,128)S(1)}, bf16[16,8,1152]{2,1,0:T(8,128)(2,1)}) custom-call(bf16[256,1024]{1,0:T(8,128)(2,1)S(1)} %bitcast.14, bf16[1024,256]{1,0:T(8,128)(2,1)S(1)} %pad_maximum_fusion.refs_1_.refs_5_, bf16[512,256]{1,0:T(8,128)(2,1)S(1)} %pad_maximum_fusion.1.refs_2_.refs_4_, ...), custom_call_target="tpu_custom_call" | custom-call | tf_op jit(solution)/shard_map/pallas_call | solution.py:263
  78.3 5.2 %all-to-all-start.2 = ((bf16[16,8,1152]{2,1,0:T(8,128)(2,1)}), bf16[16,8,1152]{2,1,0:T(8,128)(2,1)S(1)}, u32[]{:S(2)}, u32[]{:S(2)}) async-start(bf16[16,8,1152]{2,1,0:T(8,128)(2,1)} %get-tuple-element.42), calls=%async_computation.2 | async-start | bytes 589824 | tf_op jit(solution)/shard_map/all_to_all | solution.py:147
  84.2 2.4 %shard_map.196.refs_2_ = bf16[256,128]{1,0:T(8,128)(2,1)S(1)} custom-call(f32[256,128]{1,0:T(8,128)S(1)} %get-tuple-element.43.refs_0_, bf16[1024,256]{1,0:T(8,128)(2,1)S(1)} %pad_maximum_fusion.refs_1_.refs_5_, bf16[512,256]{1,0:T(8,128)(2,1)S(1)} %pad_maximum_fusion.1.refs_2_.refs_4_, bf16[512,256]{1,0:T(8,128)(2,1)S(1)} %collective-permute-done.8.refs_3_, ...), custom_call_target="tpu_custom_call" | custom-call | tf_op jit(solution)/shard_map/pallas_call | solution.py:263
  86.6 4.2 %all-to-all-done.2.refs_1_ = bf16[16,8,1152]{2,1,0:T(8,128)(2,1)S(1)} async-done(((bf16[16,8,1152]{2,1,0:T(8,128)(2,1)}), bf16[16,8,1152]{2,1,0:T(8,128)(2,1)S(1)}, u32[]{:S(2)}, u32[]{:S(2)}) %all-to-all-start.2) | async-done | bytes 294944 | tf_op jit(solution)/shard_map/all_to_all | solution.py:147
  90.8 4.2 %shard_map.197 = bf16[256,512]{1,0:T(8,128)(2,1)S(1)} custom-call(s32[16]{0:T(128)S(1)} %fusion.5.refs_0_, bf16[16,8,1152]{2,1,0:T(8,128)(2,1)S(1)} %all-to-all-done.2.refs_1_, bf16[256,128]{1,0:T(8,128)(2,1)S(1)} %shard_map.196.refs_2_, bf16[256,128]{1,0:T(8,128)(2,1)S(1)} %get-tuple-element.44.refs_3_, ...), custom_call_target="tpu_custom_call" | custom-call | tf_op jit(solution)/shard_map/pallas_call | solution.py:263
  95.1 12.5 %all_to_all.21.refs_0_.refs_5_ = bf16[8,32,512]{2,1,0:T(8,128)(2,1)S(1)} all-to-all(bf16[8,32,512]{2,1,0:T(8,128)(2,1)S(1)} %bitcast.15), channel_id=1, replica_groups=mesh['row'=8,'col'=16] {'row'}, dimensions={0} | all-to-all | bytes 524288 | tf_op jit(solution)/shard_map/all_to_all | solution.py:147
  107.6 8.3 %shard_map.198 = (bf16[512,512]{1,0:T(8,128)(2,1)S(1)}, bf16[512,256]{1,0:T(8,128)(2,1)}, bf16[96,512]{1,0:T(8,128)(2,1)S(1)}, bf16[96,512]{1,0:T(8,128)(2,1)S(1...) custom-call(bf16[8,32,512]{2,1,0:T(8,128)(2,1)S(1)} %all_to_all.21.refs_0_.refs_5_, ...), custom_call_target="tpu_custom_call" | custom-call | tf_op jit(solution)/shard_map/pallas_call | solution.py:263
  115.9 2.5 %collective-permute-start.18 = (bf16[96,512]{1,0:T(8,128)(2,1)S(1)}, bf16[96,512]{1,0:T(8,128)(2,1)S(1)}, u32[]{:S(2)}, u32[]{:S(2)}) collective-permute-start(bf16[96,512]{1,0:T(8,128)(2,1)S(1)} %get-tuple-element.49), channel_id=1, source_target_pairs={{0,16},{16,32},{32,48},{48,64},{64,80},{80,96},{96,112},{1,17},{17... | collective-permute-start | bytes 294920 | tf_op jit(solution)/shard_map/ppermute | solution.py:118
  118.3 3.6 %collective-permute-start.19 = (bf16[96,512]{1,0:T(8,128)(2,1)S(1)}, bf16[96,512]{1,0:T(8,128)(2,1)S(1)}, u32[]{:S(2)}, u32[]{:S(2)}) collective-permute-start(bf16[96,512]{1,0:T(8,128)(2,1)S(1)} %get-tuple-element.50), channel_id=1, source_target_pairs={{16,0},{32,16},{48,32},{64,48},{80,64},{96,80},{112,96},{17,1},{33... | collective-permute-start | bytes 294920 | tf_op jit(solution)/shard_map/ppermute | solution.py:118
  121.9 4.3 %shard_map.199.refs_12_ = f32[512,256]{1,0:T(8,128)S(1)} custom-call(bf16[512,256]{1,0:T(8,128)(2,1)} %get-tuple-element.47.refs_8_.refs_0_, bf16[896,256]{1,0:T(8,128)(2,1)} %get-tuple-element.51.refs_1_.refs_2_, bf16[512,512]{1,0:T(8,128)(2,1)S(1)} %get-tuple-element.52.refs_2_, bf16[896,256]{1,0:T(8,128)(2,1)} %get-tuple-element.53.refs_3_, ...), custom_call_target="tpu_custom_call" | custom-call | tf_op jit(solution)/shard_map/pallas_call | solution.py:263
  126.5 1.9 %collective-permute-start.20 = (bf16[80,512]{1,0:T(8,128)(2,1)S(1)}, bf16[80,512]{1,0:T(8,128)(2,1)S(1)}, u32[]{:S(2)}, u32[]{:S(2)}) collective-permute-start(bf16[80,512]{1,0:T(8,128)(2,1)S(1)} %get-tuple-element.65), channel_id=1, source_target_pairs={{0,1},{1,2},{2,3},{3,4},{4,5},{5,6},{6,7},{7,8},{8,9},{9,10},{10,1... | collective-permute-start | bytes 245768 | tf_op jit(solution)/shard_map/ppermute | solution.py:118
  128.4 6.0 %collective-permute-start.21 = (bf16[80,512]{1,0:T(8,128)(2,1)S(1)}, bf16[80,512]{1,0:T(8,128)(2,1)S(1)}, u32[]{:S(2)}, u32[]{:S(2)}) collective-permute-start(bf16[80,512]{1,0:T(8,128)(2,1)S(1)} %get-tuple-element.66), channel_id=1, source_target_pairs={{1,0},{2,1},{3,2},{4,3},{5,4},{6,5},{7,6},{8,7},{9,8},{10,9},{11,1... | collective-permute-start | bytes 245768 | tf_op jit(solution)/shard_map/ppermute | solution.py:118
  135.1 5.7 %shard_map.201 = (f32[512,256]{1,0:T(8,128)S(1)}, bf16[32,1024]{1,0:T(8,128)(2,1)}) custom-call(bf16[512,256]{1,0:T(8,128)(2,1)} %get-tuple-element.60.refs_9_.refs_0_, bf16[896,256]{1,0:T(8,128)(2,1)} %get-tuple-element.61.refs_1_.refs_4_, bf16[512,512]{1,0:T(8,128)(2,1)S(1)} %get-tuple-element.52.refs_2_, ...), custom_call_target="tpu_custom_call" | custom-call | tf_op jit(solution)/shard_map/pallas_call | solution.py:263
  140.8 5.7 %shard_map.202 = bf16[512,256]{1,0:T(8,128)(2,1)} custom-call(bf16[512,128]{1,0:T(8,128)(2,1)} %constant.113.clone.refs_7_.refs_0_, bf16[384,512]{1,0:T(8,128)(2,1)} %get-tuple-element.64.refs_1_, bf16[896,256]{1,0:T(8,128)(2,1)} %get-tuple-element.51.refs_1_.refs_2_, bf16[896,256]{1,0:T(8,128)(2,1)} %get-tuple-element.53.refs_3_, ...), custom_call_target="tpu_custom_call" | custom-call | tf_op jit(solution)/shard_map/pallas_call | solution.py:263
  (57 shorter events, 10.9 us)
Async XLA Ops:
  0.6 10.0 %copy-start.4 = (s32[384]{0:T(512)S(1)}, s32[384]{0:T(512)}, u32[]{:S(2)}) copy-start(s32[384]{0:T(512)} %constant.117.clone) | copy-start | bytes 4612
  0.6 10.0 %copy-start.5 = (s32[384]{0:T(512)S(1)}, s32[384]{0:T(512)}, u32[]{:S(2)}) copy-start(s32[384]{0:T(512)} %constant.116.clone) | copy-start | bytes 4612
  0.7 11.2 %copy-start = (bf16[32,96]{1,0:T(8,128)(2,1)S(1)}, bf16[32,96]{1,0:T(8,128)(2,1)}, u32[]{:S(2)}) copy-start(bf16[32,96]{1,0:T(8,128)(2,1)} %constant.114.clone.refs_0_) | copy-start | bytes 18436
  0.7 19.4 %copy-start.3 = (bf16[384,128]{1,0:T(8,128)(2,1)S(1)}, bf16[384,128]{1,0:T(8,128)(2,1)}, u32[]{:S(2)}) copy-start(bf16[384,128]{1,0:T(8,128)(2,1)} %constant.158) | copy-start | bytes 294916
  1.5 9.2 %collective-permute-start = (bf16[96,256]{1,0:T(8,128)(2,1)S(1)}, bf16[96,256]{1,0:T(8,128)(2,1)S(1)}, u32[]{:S(2)}, u32[]{:S(2)}) collective-permute-start(bf16[96,256]{1,0:T(8,128)(2,1)S(1)} %bitcast.22), channel_id=1, source_target_pairs={{0,16},{16,32},{32,48},{48,64},{64,80},{80,96},{96,112},{1,17},{17... | collective-permute-start | bytes 147464 | tf_op jit(solution)/shard_map/ppermute | solution.py:118
  5.0 6.9 %collective-permute-start.1 = (bf16[96,256]{1,0:T(8,128)(2,1)S(1)}, bf16[96,256]{1,0:T(8,128)(2,1)S(1)}, u32[]{:S(2)}, u32[]{:S(2)}) collective-permute-start(bf16[96,256]{1,0:T(8,128)(2,1)S(1)} %bitcast.21), channel_id=1, source_target_pairs={{16,0},{32,16},{48,32},{64,48},{80,64},{96,80},{112,96},{17,1},{33... | collective-permute-start | bytes 147464 | tf_op jit(solution)/shard_map/ppermute | solution.py:118
  12.1 8.8 %collective-permute-start.2 = (bf16[80,256]{1,0:T(8,128)(2,1)S(1)}, bf16[80,256]{1,0:T(8,128)(2,1)S(1)}, u32[]{:S(2)}, u32[]{:S(2)}) collective-permute-start(bf16[80,256]{1,0:T(8,128)(2,1)S(1)} %get-tuple-element.37), channel_id=1, source_target_pairs={{0,1},{1,2},{2,3},{3,4},{4,5},{5,6},{6,7},{7,8},{8,9},{9,10},{10,1... | collective-permute-start | bytes 122888 | tf_op jit(solution)/shard_map/ppermute | solution.py:118
  14.0 7.7 %collective-permute-start.3 = (bf16[80,256]{1,0:T(8,128)(2,1)S(1)}, bf16[80,256]{1,0:T(8,128)(2,1)S(1)}, u32[]{:S(2)}, u32[]{:S(2)}) collective-permute-start(bf16[80,256]{1,0:T(8,128)(2,1)S(1)} %get-tuple-element.38), channel_id=1, source_target_pairs={{1,0},{2,1},{3,2},{4,3},{5,4},{6,5},{7,6},{8,7},{9,8},{10,9},{11,1... | collective-permute-start | bytes 122888 | tf_op jit(solution)/shard_map/ppermute | solution.py:118
  31.2 28.3 %copy-start.2 = (bf16[4,8,1024]{2,1,0:T(8,128)(2,1)S(1)}, bf16[4,8,1024]{2,1,0:T(8,128)(2,1)}, u32[]{:S(2)}) copy-start(bf16[4,8,1024]{2,1,0:T(8,128)(2,1)} %param.25) | copy-start | bytes 196612
  44.0 7.9 %collective-permute-start.7 = (bf16[256,256]{1,0:T(8,128)(2,1)S(1)}, bf16[256,256]{1,0:T(8,128)(2,1)S(1)}, u32[]{:S(2)}, u32[]{:S(2)}) collective-permute-start(bf16[256,256]{1,0:T(8,128)(2,1)S(1)} %get-tuple-element.71), channel_id=1, source_target_pairs={{0,8},{1,9},{2,10},{3,11},{4,12},{5,13},{6,14},{7,15},{8,0},{9,1},... | collective-permute-start | bytes 393224 | tf_op jit(solution)/shard_map/ppermute | solution.py:111
  47.1 6.9 %collective-permute-start.6 = (bf16[256,256]{1,0:T(8,128)(2,1)S(1)}, bf16[256,256]{1,0:T(8,128)(2,1)S(1)}, u32[]{:S(2)}, u32[]{:S(2)}) collective-permute-start(bf16[256,256]{1,0:T(8,128)(2,1)S(1)} %get-tuple-element.71), channel_id=1, source_target_pairs={{0,12},{1,13},{2,14},{3,15},{4,0},{5,1},{6,2},{7,3},{8,4},{9,5},{1... | collective-permute-start | bytes 393224 | tf_op jit(solution)/shard_map/ppermute | solution.py:111
  48.1 6.3 %collective-permute-start.5 = (bf16[256,256]{1,0:T(8,128)(2,1)S(1)}, bf16[256,256]{1,0:T(8,128)(2,1)S(1)}, u32[]{:S(2)}, u32[]{:S(2)}) collective-permute-start(bf16[256,256]{1,0:T(8,128)(2,1)S(1)} %get-tuple-element.71), channel_id=1, source_target_pairs={{0,4},{1,5},{2,6},{3,7},{4,8},{5,9},{6,10},{7,11},{8,12},{9,13},{1... | collective-permute-start | bytes 393224 | tf_op jit(solution)/shard_map/ppermute | solution.py:111
  49.1 6.5 %collective-permute-start.4 = (bf16[256,256]{1,0:T(8,128)(2,1)S(1)}, bf16[256,256]{1,0:T(8,128)(2,1)S(1)}, u32[]{:S(2)}, u32[]{:S(2)}) collective-permute-start(bf16[256,256]{1,0:T(8,128)(2,1)S(1)} %get-tuple-element.72), channel_id=1, source_target_pairs={{0,2},{1,3},{2,0},{3,1},{4,6},{5,7},{6,4},{7,5},{8,10},{9,11},{10,... | collective-permute-start | bytes 393224 | tf_op jit(solution)/shard_map/ppermute | solution.py:111
  54.4 16.8 %collective-permute-start.15 = (bf16[1024,256]{1,0:T(8,128)(2,1)S(1)}, bf16[1024,256]{1,0:T(8,128)(2,1)}, u32[]{:S(2)}, u32[]{:S(2)}) collective-permute-start(bf16[1024,256]{1,0:T(8,128)(2,1)S(1)} %pad_maximum_fusion.refs_1_.refs_5_), channel_id=1, source_target_pairs={{0,2},{1,3},{2,0},{3,1},{4,6},{5,7},{6,4},{7,5},{8,10},{9,11},{10,... | collective-permute-start | bytes 1572872 | tf_op jit(solution)/shard_map/ppermute | solution.py:111
  55.6 9.4 %collective-permute-start.8 = (bf16[512,256]{1,0:T(8,128)(2,1)S(1)}, bf16[512,256]{1,0:T(8,128)(2,1)S(1)}, u32[]{:S(2)}, u32[]{:S(2)}) collective-permute-start(bf16[512,256]{1,0:T(8,128)(2,1)S(1)} %pad_maximum_fusion.1.refs_2_.refs_4_), channel_id=1, source_target_pairs={{0,4},{1,5},{2,6},{3,7},{4,8},{5,9},{6,10},{7,11},{8,12},{9,13},{1... | collective-permute-start | bytes 786440 | tf_op jit(solution)/shard_map/ppermute | solution.py:111
  57.3 9.2 %collective-permute-start.9 = (bf16[512,256]{1,0:T(8,128)(2,1)S(1)}, bf16[512,256]{1,0:T(8,128)(2,1)S(1)}, u32[]{:S(2)}, u32[]{:S(2)}) collective-permute-start(bf16[512,256]{1,0:T(8,128)(2,1)S(1)} %pad_maximum_fusion.1.refs_2_.refs_4_), channel_id=1, source_target_pairs={{0,12},{1,13},{2,14},{3,15},{4,0},{5,1},{6,2},{7,3},{8,4},{9,5},{1... | collective-permute-start | bytes 786440 | tf_op jit(solution)/shard_map/ppermute | solution.py:111
  57.7 13.0 %collective-permute-start.10 = (bf16[512,256]{1,0:T(8,128)(2,1)S(1)}, bf16[512,256]{1,0:T(8,128)(2,1)S(1)}, u32[]{:S(2)}, u32[]{:S(2)}) collective-permute-start(bf16[512,256]{1,0:T(8,128)(2,1)S(1)} %pad_maximum_fusion.1.refs_2_.refs_4_), channel_id=1, source_target_pairs={{0,8},{1,9},{2,10},{3,11},{4,12},{5,13},{6,14},{7,15},{8,0},{9,1},... | collective-permute-start | bytes 786440 | tf_op jit(solution)/shard_map/ppermute | solution.py:111
  60.3 14.8 %all-to-all-start.1 = ((bf16[8,32,1024]{2,1,0:T(8,128)(2,1)}), bf16[8,32,1024]{2,1,0:T(8,128)(2,1)S(1)}, u32[]{:S(2)}, u32[]{:S(2)}) async-start(bf16[8,32,1024]{2,1,0:T(8,128)(2,1)} %broadcast_in_dim.7), calls=%async_computation.1 | async-start | bytes 1048576 | tf_op jit(solution)/shard_map/all_to_all | solution.py:147
  65.0 18.5 %copy-start.1 = (s32[4]{0:T(128)S(1)}, s32[4]{0:T(128)}, u32[]{:S(2)}) copy-start(s32[4]{0:T(128)} %constant.119.clone) | copy-start | bytes 52
  65.0 5.7 %collective-permute-start.11 = (bf16[512,256]{1,0:T(8,128)(2,1)S(1)}, bf16[512,256]{1,0:T(8,128)(2,1)S(1)}, u32[]{:S(2)}, u32[]{:S(2)}) collective-permute-start(bf16[512,256]{1,0:T(8,128)(2,1)S(1)} %pad_maximum_fusion.1.refs_2_.refs_4_), channel_id=1, source_target_pairs={{0,1},{1,0},{2,3},{3,2},{4,5},{5,4},{6,7},{7,6},{8,9},{9,8},{10,11... | collective-permute-start | bytes 786440 | tf_op jit(solution)/shard_map/ppermute | solution.py:111
  65.0 10.1 %collective-permute-start.12 = (bf16[512,256]{1,0:T(8,128)(2,1)S(1)}, bf16[512,256]{1,0:T(8,128)(2,1)S(1)}, u32[]{:S(2)}, u32[]{:S(2)}) collective-permute-start(bf16[512,256]{1,0:T(8,128)(2,1)S(1)} %collective-permute-done.8.refs_3_), channel_id=1, source_target_pairs={{0,1},{1,0},{2,3},{3,2},{4,5},{5,4},{6,7},{7,6},{8,9},{9,8},{10,11... | collective-permute-start | bytes 786440 | tf_op jit(solution)/shard_map/ppermute | solution.py:111
  66.6 8.6 %collective-permute-start.13 = (bf16[512,256]{1,0:T(8,128)(2,1)S(1)}, bf16[512,256]{1,0:T(8,128)(2,1)S(1)}, u32[]{:S(2)}, u32[]{:S(2)}) collective-permute-start(bf16[512,256]{1,0:T(8,128)(2,1)S(1)} %collective-permute-done.9.refs_4_), channel_id=1, source_target_pairs={{0,1},{1,0},{2,3},{3,2},{4,5},{5,4},{6,7},{7,6},{8,9},{9,8},{10,11... | collective-permute-start | bytes 786440 | tf_op jit(solution)/shard_map/ppermute | solution.py:111
  70.7 4.5 %collective-permute-start.14 = (bf16[512,256]{1,0:T(8,128)(2,1)S(1)}, bf16[512,256]{1,0:T(8,128)(2,1)S(1)}, u32[]{:S(2)}, u32[]{:S(2)}) collective-permute-start(bf16[512,256]{1,0:T(8,128)(2,1)S(1)} %collective-permute-done.10.refs_5_), channel_id=1, source_target_pairs={{0,1},{1,0},{2,3},{3,2},{4,5},{5,4},{6,7},{7,6},{8,9},{9,8},{10,11... | collective-permute-start | bytes 786440 | tf_op jit(solution)/shard_map/ppermute | solution.py:111
  70.7 15.9 %collective-permute-start.16 = (bf16[1024,256]{1,0:T(8,128)(2,1)S(1)}, bf16[1024,256]{1,0:T(8,128)(2,1)}, u32[]{:S(2)}, u32[]{:S(2)}) collective-permute-start(bf16[1024,256]{1,0:T(8,128)(2,1)S(1)} %pad_maximum_fusion.refs_1_.refs_5_), channel_id=1, source_target_pairs={{0,1},{1,0},{2,3},{3,2},{4,5},{5,4},{6,7},{7,6},{8,9},{9,8},{10,11... | collective-permute-start | bytes 1572872 | tf_op jit(solution)/shard_map/ppermute | solution.py:111
  71.2 19.6 %collective-permute-start.17 = (bf16[1024,256]{1,0:T(8,128)(2,1)}, bf16[1024,256]{1,0:T(8,128)(2,1)}, u32[]{:S(2)}, u32[]{:S(2)}) collective-permute-start(bf16[1024,256]{1,0:T(8,128)(2,1)} %collective-permute-done.15.refs_6_), channel_id=1, source_target_pairs={{0,1},{1,0},{2,3},{3,2},{4,5},{5,4},{6,7},{7,6},{8,9},{9,8},{10,11... | collective-permute-start | bytes 1572872 | tf_op jit(solution)/shard_map/ppermute | solution.py:111
  78.3 12.6 %all-to-all-start.2 = ((bf16[16,8,1152]{2,1,0:T(8,128)(2,1)}), bf16[16,8,1152]{2,1,0:T(8,128)(2,1)S(1)}, u32[]{:S(2)}, u32[]{:S(2)}) async-start(bf16[16,8,1152]{2,1,0:T(8,128)(2,1)} %get-tuple-element.42), calls=%async_computation.2 | async-start | bytes 589824 | tf_op jit(solution)/shard_map/all_to_all | solution.py:147
  115.9 10.4 %collective-permute-start.18 = (bf16[96,512]{1,0:T(8,128)(2,1)S(1)}, bf16[96,512]{1,0:T(8,128)(2,1)S(1)}, u32[]{:S(2)}, u32[]{:S(2)}) collective-permute-start(bf16[96,512]{1,0:T(8,128)(2,1)S(1)} %get-tuple-element.49), channel_id=1, source_target_pairs={{0,16},{16,32},{32,48},{48,64},{64,80},{80,96},{96,112},{1,17},{17... | collective-permute-start | bytes 294920 | tf_op jit(solution)/shard_map/ppermute | solution.py:118
  118.3 7.9 %collective-permute-start.19 = (bf16[96,512]{1,0:T(8,128)(2,1)S(1)}, bf16[96,512]{1,0:T(8,128)(2,1)S(1)}, u32[]{:S(2)}, u32[]{:S(2)}) collective-permute-start(bf16[96,512]{1,0:T(8,128)(2,1)S(1)} %get-tuple-element.50), channel_id=1, source_target_pairs={{16,0},{32,16},{48,32},{64,48},{80,64},{96,80},{112,96},{17,1},{33... | collective-permute-start | bytes 294920 | tf_op jit(solution)/shard_map/ppermute | solution.py:118
  126.5 14.3 %collective-permute-start.20 = (bf16[80,512]{1,0:T(8,128)(2,1)S(1)}, bf16[80,512]{1,0:T(8,128)(2,1)S(1)}, u32[]{:S(2)}, u32[]{:S(2)}) collective-permute-start(bf16[80,512]{1,0:T(8,128)(2,1)S(1)} %get-tuple-element.65), channel_id=1, source_target_pairs={{0,1},{1,2},{2,3},{3,4},{4,5},{5,6},{6,7},{7,8},{8,9},{9,10},{10,1... | collective-permute-start | bytes 245768 | tf_op jit(solution)/shard_map/ppermute | solution.py:118
  128.4 12.4 %collective-permute-start.21 = (bf16[80,512]{1,0:T(8,128)(2,1)S(1)}, bf16[80,512]{1,0:T(8,128)(2,1)S(1)}, u32[]{:S(2)}, u32[]{:S(2)}) collective-permute-start(bf16[80,512]{1,0:T(8,128)(2,1)S(1)} %get-tuple-element.66), channel_id=1, source_target_pairs={{1,0},{2,1},{3,2},{4,3},{5,4},{6,5},{7,6},{8,7},{9,8},{10,9},{11,1... | collective-permute-start | bytes 245768 | tf_op jit(solution)/shard_map/ppermute | solution.py:118

commit v2 on v1

--- a/solution.py
+++ b/solution.py
@@ -391,12 +391,12 @@
         out = dot(weight, v_out[:, to])
         norm = out[:, DELTA_LANE : DELTA_LANE + 1]
         q_out[:, to] = at_lanes(q, lane, LSE_LANE, top + jnp.log(norm)).astype(bf16)
-        out = jnp.where(channel, out / norm, 0.0)
-        a0_out[:, at] = out.astype(bf16)
-        outs.append(out)
+        outs.append(out / norm)
+    a0 = as_pairs(outs)
+    a0_out[...] = a0
     for result in (q_one, q_two, k_one, k_two, v_one, v_two, q_halo_out, a0_out):
         result.send()
-    y = (x + dot(as_pairs(outs), w_out_ref[...])).astype(bf16)
+    y = (x + dot(a0, w_out_ref[...])).astype(bf16)
     quarter = own // 4
     m1 = dot(y[:quarter], one_ref[:C0])
     for part in range(1, 4):
@@ -528,12 +528,13 @@
     dy_out[...] = dy
     dy_out.send()
     da0 = dot_last(dy, w_out_ref[...]).astype(bf16).astype(f32)
+    a0 = a0_ref[...].astype(f32)
     lane = lax.broadcasted_iota(jnp.int32, (1, LANES), 1)
     is_lse = (lane == LSE_LANE) | (lane == LSE_LANE + 1)
     for h in range(NA_HEADS):
         at = head_lanes(h)
         mine = jnp.where(lane < NA_DIM, head_of(da0, h), 0.0)
-        delta = jnp.sum(mine * a0_ref[:, at].astype(f32), -1, keepdims=True)
+        delta = jnp.sum(mine * head_of(a0, h), -1, keepdims=True)
         q_ref = q_two if h // 2 else q_one
         mine = jnp.where(is_lse, q_ref[:, head_lanes(h % 2)].astype(f32), mine)
         dout_out[:, at] = at_lanes(mine, lane, DELTA_LANE, delta).astype(bf16)
@@ -565,6 +566,11 @@
     dxn = through_projection(dq, 0, heads[0], w_ref)
     dxn += through_projection(dk, 1, heads[0], w_ref)
     dxn_out[...] = dxn + through_projection(dv, 2, heads[0], w_ref)
+
+
+def na_first_kernel(heads, q_ref, k_ref, dout_ref, v_ref, w_ref, part_ref, dxn_out, grad_out):
+    na_own_kernel(heads, q_ref, k_ref, dout_ref, v_ref, w_ref, dxn_out)
+    grad_out[...] = jnp.sum(part_ref[:, :, :C2].astype(f32), 0)
 
 
 def na_rest_kernel(
@@ -693,7 +699,7 @@
             ((own + padded, WIDE // 2), bf16),
             ((own + padded, WIDE // 2), bf16),
             ((padded, WIDE), bf16),
-            ((own, WIDE), bf16),
+            ((own, C0), bf16),
         ],
         (
             flat,
@@ -750,7 +756,6 @@
         scratch=(pltpu.VMEM((1, part), f32), pltpu.VMEM((1, part), f32)),
         smem=1,
     )[0]
-    grad_wo = jnp.sum(shares[:, :, :C2].astype(f32), 0)
     back = all_to_all(back.reshape(n_row, tokens, 4 * dim), "row")
 
     dout0, dy0, top, bottom, left, right = call(
@@ -765,12 +770,12 @@
     )
     before, after = row_halo(top, bottom)
     half = NA_HEADS // 2
-    dxn_one = call(
-        functools.partial(na_own_kernel, range(half)),
-        [((own, C0), f32)],
-        (q_one, k_one, dout0, v_one, na_qkv),
-        manual=(0, 1, 3, 4),
-    )[0]
+    dxn_one, grad_wo = call(
+        functools.partial(na_first_kernel, range(half)),
+        [((own, C0), f32), ((dim // n_col, C2), f32)],
+        (q_one, k_one, dout0, v_one, na_qkv, shares),
+        manual=(0, 1, 3, 4, 5),
+    )
     before, after, dxn_one = lax.optimization_barrier((before, after, dxn_one))
     left, right = call(
         corner_kernel,

time: 147 us -> 148 us (level)
  no operation moved by 1% of the time
where the time goes in v2:
time: 148 us; the launch traced here: 147 us
  starting transfers between devices  49 us (33%)
  Pallas kernels  44.3 us (30%)
  blocking collectives  25.3 us (17%)
  waiting for transfers between devices  20.5 us (14%)
  local copies, waits for them, and re-layouts  3.43 us (2%)
  matrix products  2.34 us (2%)
    pallas_call x10, Pallas kernels, call(): pl.pallas_call(body, out_shape=[pltpu.HBM(*out) if i in out_manual else j...  44.3 us
    all_to_all x2, blocking collectives, all_to_all(): return lax.all_to_all(array, axis, split_axis=0, concat_axis=0, tiled=True)  25.3 us
    ppermute x4, starting transfers between devices, neighbours(): lax.ppermute(to_previous, axis, down)  18.1 us
    ppermute x14, starting transfers between devices, shifted(): return lax.ppermute(array, axis, [(i, move(i)) for i in range(count)])  11.2 us
    ppermute x14, waiting for transfers between devices, shifted(): return lax.ppermute(array, axis, [(i, move(i)) for i in range(count)])  10.6 us
    all_to_all x2, starting transfers between devices, all_to_all(): return lax.all_to_all(array, axis, split_axis=0, concat_axis=0, tiled=True)  9.92 us
    ppermute x4, starting transfers between devices, neighbours(): lax.ppermute(to_next, axis, up)  9.76 us
    all_to_all x2, waiting for transfers between devices, all_to_all(): return lax.all_to_all(array, axis, split_axis=0, concat_axis=0, tiled=True)  7.88 us
  transfers between devices with their start and end apart: 24, of which 10 were waited for; matrix products, arithmetic and copies ran while one was open for 4% of the time, Pallas kernels for 11%

profile of v2, /device:TPU:34, one launch (start us, length us, event | category | flops | bytes accessed | tf_op | source)
XLA Modules:
  0.0 146.9 jit_solution(15392999877383861677)
XLA Ops:
  1.5 3.4 %collective-permute-start = (bf16[96,256]{1,0:T(8,128)(2,1)S(1)}, bf16[96,256]{1,0:T(8,128)(2,1)S(1)}, u32[]{:S(2)}, u32[]{:S(2)}) collective-permute-start(bf16[96,256]{1,0:T(8,128)(2,1)S(1)} %bitcast.22), channel_id=1, source_target_pairs={{0,16},{16,32},{32,48},{48,64},{64,80},{80,96},{96,112},{1,17},{17... | collective-permute-start | bytes 147464 | tf_op jit(solution)/shard_map/ppermute | solution.py:118
  5.0 2.4 %collective-permute-start.1 = (bf16[96,256]{1,0:T(8,128)(2,1)S(1)}, bf16[96,256]{1,0:T(8,128)(2,1)S(1)}, u32[]{:S(2)}, u32[]{:S(2)}) collective-permute-start(bf16[96,256]{1,0:T(8,128)(2,1)S(1)} %bitcast.21), channel_id=1, source_target_pairs={{16,0},{32,16},{48,32},{64,48},{80,64},{96,80},{112,96},{17,1},{33... | collective-permute-start | bytes 147464 | tf_op jit(solution)/shard_map/ppermute | solution.py:118
  8.3 2.3 %convolution_convert_fusion.refs_14_ = bf16[32,1024]{1,0:T(8,128)(2,1)S(1)} fusion(bf16[1024,1024]{1,0:T(8,128)(2,1)} %refs_6_.3, bf16[4,8,1024]{2,1,0:T(8,128)(2,1)} %param.25), kind=kOutput, calls=%fused_computation.1 | convolution fusion | flops 67141632 | bytes 2228224 | tf_op jit(solution)/shard_map/dot_general | solution.py:37
  10.8 1.1 collective-permute-done.1.refs_2_.refs_4_
  12.1 1.9 %collective-permute-start.2 = (bf16[80,256]{1,0:T(8,128)(2,1)S(1)}, bf16[80,256]{1,0:T(8,128)(2,1)S(1)}, u32[]{:S(2)}, u32[]{:S(2)}) collective-permute-start(bf16[80,256]{1,0:T(8,128)(2,1)S(1)} %get-tuple-element.39), channel_id=1, source_target_pairs={{0,1},{1,2},{2,3},{3,4},{4,5},{5,6},{6,7},{7,8},{8,9},{9,10},{10,1... | collective-permute-start | bytes 122888 | tf_op jit(solution)/shard_map/ppermute | solution.py:118
  14.0 6.0 %collective-permute-start.3 = (bf16[80,256]{1,0:T(8,128)(2,1)S(1)}, bf16[80,256]{1,0:T(8,128)(2,1)S(1)}, u32[]{:S(2)}, u32[]{:S(2)}) collective-permute-start(bf16[80,256]{1,0:T(8,128)(2,1)S(1)} %get-tuple-element.40), channel_id=1, source_target_pairs={{1,0},{2,1},{3,2},{4,3},{5,4},{6,5},{7,6},{8,7},{9,8},{10,9},{11,1... | collective-permute-start | bytes 122888 | tf_op jit(solution)/shard_map/ppermute | solution.py:118
  21.7 9.5 %shard_map.194 = (bf16[8,32,512]{2,1,0:T(8,128)(2,1)S(1)}, bf16[32,1024]{1,0:T(8,128)(2,1)}, bf16[512,256]{1,0:T(8,128)(2,1)}, bf16[512,256]{1,0:T(8,128)(2,1)},...) custom-call(bf16[512,256]{1,0:T(8,128)(2,1)} %bitcast.17, ...), custom_call_target="tpu_custom_call" | custom-call | tf_op jit(solution)/shard_map/pallas_call | solution.py:263
  31.2 12.8 %all_to_all.20 = bf16[8,32,512]{2,1,0:T(8,128)(2,1)S(1)} all-to-all(bf16[8,32,512]{2,1,0:T(8,128)(2,1)S(1)} %get-tuple-element.41), channel_id=1, replica_groups=mesh['row'=8,'col'=16] {'row'}, dimensions={0} | all-to-all | bytes 524288 | tf_op jit(solution)/shard_map/all_to_all | solution.py:147
  44.0 3.0 %collective-permute-start.7 = (bf16[256,256]{1,0:T(8,128)(2,1)S(1)}, bf16[256,256]{1,0:T(8,128)(2,1)S(1)}, u32[]{:S(2)}, u32[]{:S(2)}) collective-permute-start(bf16[256,256]{1,0:T(8,128)(2,1)S(1)} %get-tuple-element.75), channel_id=1, source_target_pairs={{0,8},{1,9},{2,10},{3,11},{4,12},{5,13},{6,14},{7,15},{8,0},{9,1},... | collective-permute-start | bytes 393224 | tf_op jit(solution)/shard_map/ppermute | solution.py:111
  48.0 1.0 collective-permute-start.5
  49.5 2.4 %collective-permute-done.7 = bf16[256,256]{1,0:T(8,128)(2,1)S(1)} collective-permute-done((bf16[256,256]{1,0:T(8,128)(2,1)S(1)}, bf16[256,256]{1,0:T(8,128)(2,1)S(1)}, u32[]{:S(2)}, u32[]{:S(2)}) %collective-permute-start.7) | collective-permute-done | bytes 131104 | tf_op jit(solution)/shard_map/ppermute | solution.py:111
  51.9 2.0 %collective-permute-done.6 = bf16[256,256]{1,0:T(8,128)(2,1)S(1)} collective-permute-done((bf16[256,256]{1,0:T(8,128)(2,1)S(1)}, bf16[256,256]{1,0:T(8,128)(2,1)S(1)}, u32[]{:S(2)}, u32[]{:S(2)}) %collective-permute-start.6) | collective-permute-done | bytes 131104 | tf_op jit(solution)/shard_map/ppermute | solution.py:111
  55.6 1.7 %collective-permute-start.8 = (bf16[512,256]{1,0:T(8,128)(2,1)S(1)}, bf16[512,256]{1,0:T(8,128)(2,1)S(1)}, u32[]{:S(2)}, u32[]{:S(2)}) collective-permute-start(bf16[512,256]{1,0:T(8,128)(2,1)S(1)} %pad_maximum_fusion.1.refs_2_.refs_4_), channel_id=1, source_target_pairs={{0,4},{1,5},{2,6},{3,7},{4,8},{5,9},{6,10},{7,11},{8,12},{9,13},{1... | collective-permute-start | bytes 786440 | tf_op jit(solution)/shard_map/ppermute | solution.py:111
  57.7 1.8 %collective-permute-start.10 = (bf16[512,256]{1,0:T(8,128)(2,1)S(1)}, bf16[512,256]{1,0:T(8,128)(2,1)S(1)}, u32[]{:S(2)}, u32[]{:S(2)}) collective-permute-start(bf16[512,256]{1,0:T(8,128)(2,1)S(1)} %pad_maximum_fusion.1.refs_2_.refs_4_), channel_id=1, source_target_pairs={{0,8},{1,9},{2,10},{3,11},{4,12},{5,13},{6,14},{7,15},{8,0},{9,1},... | collective-permute-start | bytes 786440 | tf_op jit(solution)/shard_map/ppermute | solution.py:111
  60.3 4.7 %all-to-all-start.1 = ((bf16[8,32,1024]{2,1,0:T(8,128)(2,1)}), bf16[8,32,1024]{2,1,0:T(8,128)(2,1)S(1)}, u32[]{:S(2)}, u32[]{:S(2)}) async-start(bf16[8,32,1024]{2,1,0:T(8,128)(2,1)} %broadcast_in_dim.7), calls=%async_computation.1 | async-start | bytes 1048576 | tf_op jit(solution)/shard_map/all_to_all | solution.py:147
  65.5 1.0 collective-permute-done.9.refs_4_
  66.5 4.1 %collective-permute-done.10.refs_5_ = bf16[512,256]{1,0:T(8,128)(2,1)S(1)} collective-permute-done((bf16[512,256]{1,0:T(8,128)(2,1)S(1)}, bf16[512,256]{1,0:T(8,128)(2,1)S(1)}, u32[]{:S(2)}, u32[]{:S(2)}) %collective-permute-start.10) | collective-permute-done | bytes 262176 | tf_op jit(solution)/shard_map/ppermute | solution.py:111
  71.5 3.7 %all-to-all-done.1 = bf16[8,32,1024]{2,1,0:T(8,128)(2,1)S(1)} async-done(((bf16[8,32,1024]{2,1,0:T(8,128)(2,1)}), bf16[8,32,1024]{2,1,0:T(8,128)(2,1)S(1)}, u32[]{:S(2)}, u32[]{:S(2)}) %all-to-all-start.1) | async-done | bytes 524320 | tf_op jit(solution)/shard_map/all_to_all | solution.py:147
  75.2 3.1 %shard_map.195 = (bf16[256,128]{1,0:T(8,128)(2,1)S(1)}, f32[256,128]{1,0:T(8,128)S(1)}, bf16[16,8,1152]{2,1,0:T(8,128)(2,1)}) custom-call(bf16[256,1024]{1,0:T(8,128)(2,1)S(1)} %bitcast.14, bf16[1024,256]{1,0:T(8,128)(2,1)S(1)} %pad_maximum_fusion.refs_1_.refs_5_, bf16[512,256]{1,0:T(8,128)(2,1)S(1)} %pad_maximum_fusion.1.refs_2_.refs_4_, ...), custom_call_target="tpu_custom_call" | custom-call | tf_op jit(solution)/shard_map/pallas_call | solution.py:263
  78.2 5.2 %all-to-all-start.2 = ((bf16[16,8,1152]{2,1,0:T(8,128)(2,1)}), bf16[16,8,1152]{2,1,0:T(8,128)(2,1)S(1)}, u32[]{:S(2)}, u32[]{:S(2)}) async-start(bf16[16,8,1152]{2,1,0:T(8,128)(2,1)} %get-tuple-element.44), calls=%async_computation.2 | async-start | bytes 589824 | tf_op jit(solution)/shard_map/all_to_all | solution.py:147
  84.2 2.4 %shard_map.196.refs_2_ = bf16[256,128]{1,0:T(8,128)(2,1)S(1)} custom-call(f32[256,128]{1,0:T(8,128)S(1)} %get-tuple-element.45.refs_0_, bf16[1024,256]{1,0:T(8,128)(2,1)S(1)} %pad_maximum_fusion.refs_1_.refs_5_, bf16[512,256]{1,0:T(8,128)(2,1)S(1)} %pad_maximum_fusion.1.refs_2_.refs_4_, bf16[512,256]{1,0:T(8,128)(2,1)S(1)} %collective-permute-done.8.refs_3_, ...), custom_call_target="tpu_custom_call" | custom-call | tf_op jit(solution)/shard_map/pallas_call | solution.py:263
  86.6 4.2 %all-to-all-done.2.refs_1_.refs_5_ = bf16[16,8,1152]{2,1,0:T(8,128)(2,1)S(1)} async-done(((bf16[16,8,1152]{2,1,0:T(8,128)(2,1)}), bf16[16,8,1152]{2,1,0:T(8,128)(2,1)S(1)}, u32[]{:S(2)}, u32[]{:S(2)}) %all-to-all-start.2) | async-done | bytes 294944 | tf_op jit(solution)/shard_map/all_to_all | solution.py:147
  90.8 4.3 %shard_map.197 = bf16[256,512]{1,0:T(8,128)(2,1)S(1)} custom-call(s32[16]{0:T(128)S(1)} %fusion.5.refs_0_, bf16[16,8,1152]{2,1,0:T(8,128)(2,1)S(1)} %all-to-all-done.2.refs_1_.refs_5_, bf16[256,128]{1,0:T(8,128)(2,1)S(1)} %shard_map.196.refs_2_, bf16[256,128]{1,0:T(8,128)(2,1)S(1)} %get-tuple-element.46.refs_3_, ...), custom_call_target="tpu_custom_call" | custom-call | tf_op jit(solution)/shard_map/pallas_call | solution.py:263
  95.1 12.5 %all_to_all.21.refs_0_.refs_5_ = bf16[8,32,512]{2,1,0:T(8,128)(2,1)S(1)} all-to-all(bf16[8,32,512]{2,1,0:T(8,128)(2,1)S(1)} %bitcast.15), channel_id=1, replica_groups=mesh['row'=8,'col'=16] {'row'}, dimensions={0} | all-to-all | bytes 524288 | tf_op jit(solution)/shard_map/all_to_all | solution.py:147
  107.7 8.3 %shard_map.198 = (bf16[512,512]{1,0:T(8,128)(2,1)S(1)}, bf16[512,256]{1,0:T(8,128)(2,1)}, bf16[96,512]{1,0:T(8,128)(2,1)S(1)}, bf16[96,512]{1,0:T(8,128)(2,1)S(1...) custom-call(bf16[8,32,512]{2,1,0:T(8,128)(2,1)S(1)} %all_to_all.21.refs_0_.refs_5_, ...), custom_call_target="tpu_custom_call" | custom-call | tf_op jit(solution)/shard_map/pallas_call | solution.py:263
  116.0 2.5 %collective-permute-start.18 = (bf16[96,512]{1,0:T(8,128)(2,1)S(1)}, bf16[96,512]{1,0:T(8,128)(2,1)S(1)}, u32[]{:S(2)}, u32[]{:S(2)}) collective-permute-start(bf16[96,512]{1,0:T(8,128)(2,1)S(1)} %get-tuple-element.51), channel_id=1, source_target_pairs={{0,16},{16,32},{32,48},{48,64},{64,80},{80,96},{96,112},{1,17},{17... | collective-permute-start | bytes 294920 | tf_op jit(solution)/shard_map/ppermute | solution.py:118
  118.5 3.6 %collective-permute-start.19 = (bf16[96,512]{1,0:T(8,128)(2,1)S(1)}, bf16[96,512]{1,0:T(8,128)(2,1)S(1)}, u32[]{:S(2)}, u32[]{:S(2)}) collective-permute-start(bf16[96,512]{1,0:T(8,128)(2,1)S(1)} %get-tuple-element.52), channel_id=1, source_target_pairs={{16,0},{32,16},{48,32},{64,48},{80,64},{96,80},{112,96},{17,1},{33... | collective-permute-start | bytes 294920 | tf_op jit(solution)/shard_map/ppermute | solution.py:118
  122.1 5.0 %shard_map.199 = (f32[512,256]{1,0:T(8,128)S(1)}, f32[8,1024]{1,0:T(8,128)}) custom-call(bf16[512,256]{1,0:T(8,128)(2,1)} %get-tuple-element.49.refs_8_.refs_0_, bf16[896,256]{1,0:T(8,128)(2,1)} %get-tuple-element.53.refs_1_.refs_2_, bf16[512,512]{1,0:T(8,128)(2,1)S(1)} %get-tuple-element.54.refs_2_, bf16[896,256]{1,0:T(8,128)(2,1)} %get-tuple-element.55.refs_3_, ...), custom_call_target="tpu_custom_call" | custom-call | tf_op jit(solution)/shard_map/pallas_call | solution.py:263
  127.3 1.9 %collective-permute-start.20 = (bf16[80,512]{1,0:T(8,128)(2,1)S(1)}, bf16[80,512]{1,0:T(8,128)(2,1)S(1)}, u32[]{:S(2)}, u32[]{:S(2)}) collective-permute-start(bf16[80,512]{1,0:T(8,128)(2,1)S(1)} %get-tuple-element.68), channel_id=1, source_target_pairs={{0,1},{1,2},{2,3},{3,4},{4,5},{5,6},{6,7},{7,8},{8,9},{9,10},{10,1... | collective-permute-start | bytes 245768 | tf_op jit(solution)/shard_map/ppermute | solution.py:118
  129.2 6.0 %collective-permute-start.21 = (bf16[80,512]{1,0:T(8,128)(2,1)S(1)}, bf16[80,512]{1,0:T(8,128)(2,1)S(1)}, u32[]{:S(2)}, u32[]{:S(2)}) collective-permute-start(bf16[80,512]{1,0:T(8,128)(2,1)S(1)} %get-tuple-element.69), channel_id=1, source_target_pairs={{1,0},{2,1},{3,2},{4,3},{5,4},{6,5},{7,6},{8,7},{9,8},{10,9},{11,1... | collective-permute-start | bytes 245768 | tf_op jit(solution)/shard_map/ppermute | solution.py:118
  135.3 5.7 %shard_map.201 = (f32[512,256]{1,0:T(8,128)S(1)}, bf16[32,1024]{1,0:T(8,128)(2,1)}) custom-call(bf16[512,256]{1,0:T(8,128)(2,1)} %get-tuple-element.63.refs_9_.refs_0_, bf16[896,256]{1,0:T(8,128)(2,1)} %get-tuple-element.64.refs_1_.refs_4_, bf16[512,512]{1,0:T(8,128)(2,1)S(1)} %get-tuple-element.54.refs_2_, ...), custom_call_target="tpu_custom_call" | custom-call | tf_op jit(solution)/shard_map/pallas_call | solution.py:263
  141.0 5.7 %shard_map.202 = bf16[512,256]{1,0:T(8,128)(2,1)} custom-call(bf16[512,128]{1,0:T(8,128)(2,1)} %constant.111.clone.refs_7_.refs_0_, bf16[384,512]{1,0:T(8,128)(2,1)} %get-tuple-element.67.refs_1_, bf16[896,256]{1,0:T(8,128)(2,1)} %get-tuple-element.53.refs_1_.refs_2_, bf16[896,256]{1,0:T(8,128)(2,1)} %get-tuple-element.55.refs_3_, ...), custom_call_target="tpu_custom_call" | custom-call | tf_op jit(solution)/shard_map/pallas_call | solution.py:263
  (58 shorter events, 10.2 us)
Async XLA Ops:
  0.6 10.0 %copy-start.5 = (s32[384]{0:T(512)S(1)}, s32[384]{0:T(512)}, u32[]{:S(2)}) copy-start(s32[384]{0:T(512)} %constant.115.clone) | copy-start | bytes 4612
  0.6 10.0 %copy-start.6 = (s32[384]{0:T(512)S(1)}, s32[384]{0:T(512)}, u32[]{:S(2)}) copy-start(s32[384]{0:T(512)} %constant.114.clone) | copy-start | bytes 4612
  0.7 11.2 %copy-start.1 = (bf16[32,96]{1,0:T(8,128)(2,1)S(1)}, bf16[32,96]{1,0:T(8,128)(2,1)}, u32[]{:S(2)}) copy-start(bf16[32,96]{1,0:T(8,128)(2,1)} %constant.112.clone.refs_0_) | copy-start | bytes 18436
  0.7 19.4 %copy-start.4 = (bf16[384,128]{1,0:T(8,128)(2,1)S(1)}, bf16[384,128]{1,0:T(8,128)(2,1)}, u32[]{:S(2)}) copy-start(bf16[384,128]{1,0:T(8,128)(2,1)} %constant.156) | copy-start | bytes 294916
  1.5 9.2 %collective-permute-start = (bf16[96,256]{1,0:T(8,128)(2,1)S(1)}, bf16[96,256]{1,0:T(8,128)(2,1)S(1)}, u32[]{:S(2)}, u32[]{:S(2)}) collective-permute-start(bf16[96,256]{1,0:T(8,128)(2,1)S(1)} %bitcast.22), channel_id=1, source_target_pairs={{0,16},{16,32},{32,48},{48,64},{64,80},{80,96},{96,112},{1,17},{17... | collective-permute-start | bytes 147464 | tf_op jit(solution)/shard_map/ppermute | solution.py:118
  5.0 6.9 %collective-permute-start.1 = (bf16[96,256]{1,0:T(8,128)(2,1)S(1)}, bf16[96,256]{1,0:T(8,128)(2,1)S(1)}, u32[]{:S(2)}, u32[]{:S(2)}) collective-permute-start(bf16[96,256]{1,0:T(8,128)(2,1)S(1)} %bitcast.21), channel_id=1, source_target_pairs={{16,0},{32,16},{48,32},{64,48},{80,64},{96,80},{112,96},{17,1},{33... | collective-permute-start | bytes 147464 | tf_op jit(solution)/shard_map/ppermute | solution.py:118
  12.1 8.8 %collective-permute-start.2 = (bf16[80,256]{1,0:T(8,128)(2,1)S(1)}, bf16[80,256]{1,0:T(8,128)(2,1)S(1)}, u32[]{:S(2)}, u32[]{:S(2)}) collective-permute-start(bf16[80,256]{1,0:T(8,128)(2,1)S(1)} %get-tuple-element.39), channel_id=1, source_target_pairs={{0,1},{1,2},{2,3},{3,4},{4,5},{5,6},{6,7},{7,8},{8,9},{9,10},{10,1... | collective-permute-start | bytes 122888 | tf_op jit(solution)/shard_map/ppermute | solution.py:118
  14.0 7.7 %collective-permute-start.3 = (bf16[80,256]{1,0:T(8,128)(2,1)S(1)}, bf16[80,256]{1,0:T(8,128)(2,1)S(1)}, u32[]{:S(2)}, u32[]{:S(2)}) collective-permute-start(bf16[80,256]{1,0:T(8,128)(2,1)S(1)} %get-tuple-element.40), channel_id=1, source_target_pairs={{1,0},{2,1},{3,2},{4,3},{5,4},{6,5},{7,6},{8,7},{9,8},{10,9},{11,1... | collective-permute-start | bytes 122888 | tf_op jit(solution)/shard_map/ppermute | solution.py:118
  31.2 28.3 %copy-start.3 = (bf16[4,8,1024]{2,1,0:T(8,128)(2,1)S(1)}, bf16[4,8,1024]{2,1,0:T(8,128)(2,1)}, u32[]{:S(2)}) copy-start(bf16[4,8,1024]{2,1,0:T(8,128)(2,1)} %param.25) | copy-start | bytes 196612
  44.0 7.9 %collective-permute-start.7 = (bf16[256,256]{1,0:T(8,128)(2,1)S(1)}, bf16[256,256]{1,0:T(8,128)(2,1)S(1)}, u32[]{:S(2)}, u32[]{:S(2)}) collective-permute-start(bf16[256,256]{1,0:T(8,128)(2,1)S(1)} %get-tuple-element.75), channel_id=1, source_target_pairs={{0,8},{1,9},{2,10},{3,11},{4,12},{5,13},{6,14},{7,15},{8,0},{9,1},... | collective-permute-start | bytes 393224 | tf_op jit(solution)/shard_map/ppermute | solution.py:111
  47.0 6.9 %collective-permute-start.6 = (bf16[256,256]{1,0:T(8,128)(2,1)S(1)}, bf16[256,256]{1,0:T(8,128)(2,1)S(1)}, u32[]{:S(2)}, u32[]{:S(2)}) collective-permute-start(bf16[256,256]{1,0:T(8,128)(2,1)S(1)} %get-tuple-element.75), channel_id=1, source_target_pairs={{0,12},{1,13},{2,14},{3,15},{4,0},{5,1},{6,2},{7,3},{8,4},{9,5},{1... | collective-permute-start | bytes 393224 | tf_op jit(solution)/shard_map/ppermute | solution.py:111
  48.0 6.3 %collective-permute-start.5 = (bf16[256,256]{1,0:T(8,128)(2,1)S(1)}, bf16[256,256]{1,0:T(8,128)(2,1)S(1)}, u32[]{:S(2)}, u32[]{:S(2)}) collective-permute-start(bf16[256,256]{1,0:T(8,128)(2,1)S(1)} %get-tuple-element.75), channel_id=1, source_target_pairs={{0,4},{1,5},{2,6},{3,7},{4,8},{5,9},{6,10},{7,11},{8,12},{9,13},{1... | collective-permute-start | bytes 393224 | tf_op jit(solution)/shard_map/ppermute | solution.py:111
  49.1 6.5 %collective-permute-start.4 = (bf16[256,256]{1,0:T(8,128)(2,1)S(1)}, bf16[256,256]{1,0:T(8,128)(2,1)S(1)}, u32[]{:S(2)}, u32[]{:S(2)}) collective-permute-start(bf16[256,256]{1,0:T(8,128)(2,1)S(1)} %get-tuple-element.76), channel_id=1, source_target_pairs={{0,2},{1,3},{2,0},{3,1},{4,6},{5,7},{6,4},{7,5},{8,10},{9,11},{10,... | collective-permute-start | bytes 393224 | tf_op jit(solution)/shard_map/ppermute | solution.py:111
  54.4 16.8 %collective-permute-start.15 = (bf16[1024,256]{1,0:T(8,128)(2,1)S(1)}, bf16[1024,256]{1,0:T(8,128)(2,1)}, u32[]{:S(2)}, u32[]{:S(2)}) collective-permute-start(bf16[1024,256]{1,0:T(8,128)(2,1)S(1)} %pad_maximum_fusion.refs_1_.refs_5_), channel_id=1, source_target_pairs={{0,2},{1,3},{2,0},{3,1},{4,6},{5,7},{6,4},{7,5},{8,10},{9,11},{10,... | collective-permute-start | bytes 1572872 | tf_op jit(solution)/shard_map/ppermute | solution.py:111
  55.6 9.4 %collective-permute-start.8 = (bf16[512,256]{1,0:T(8,128)(2,1)S(1)}, bf16[512,256]{1,0:T(8,128)(2,1)S(1)}, u32[]{:S(2)}, u32[]{:S(2)}) collective-permute-start(bf16[512,256]{1,0:T(8,128)(2,1)S(1)} %pad_maximum_fusion.1.refs_2_.refs_4_), channel_id=1, source_target_pairs={{0,4},{1,5},{2,6},{3,7},{4,8},{5,9},{6,10},{7,11},{8,12},{9,13},{1... | collective-permute-start | bytes 786440 | tf_op jit(solution)/shard_map/ppermute | solution.py:111
  57.3 9.2 %collective-permute-start.9 = (bf16[512,256]{1,0:T(8,128)(2,1)S(1)}, bf16[512,256]{1,0:T(8,128)(2,1)S(1)}, u32[]{:S(2)}, u32[]{:S(2)}) collective-permute-start(bf16[512,256]{1,0:T(8,128)(2,1)S(1)} %pad_maximum_fusion.1.refs_2_.refs_4_), channel_id=1, source_target_pairs={{0,12},{1,13},{2,14},{3,15},{4,0},{5,1},{6,2},{7,3},{8,4},{9,5},{1... | collective-permute-start | bytes 786440 | tf_op jit(solution)/shard_map/ppermute | solution.py:111
  57.7 13.0 %collective-permute-start.10 = (bf16[512,256]{1,0:T(8,128)(2,1)S(1)}, bf16[512,256]{1,0:T(8,128)(2,1)S(1)}, u32[]{:S(2)}, u32[]{:S(2)}) collective-permute-start(bf16[512,256]{1,0:T(8,128)(2,1)S(1)} %pad_maximum_fusion.1.refs_2_.refs_4_), channel_id=1, source_target_pairs={{0,8},{1,9},{2,10},{3,11},{4,12},{5,13},{6,14},{7,15},{8,0},{9,1},... | collective-permute-start | bytes 786440 | tf_op jit(solution)/shard_map/ppermute | solution.py:111
  60.3 14.9 %all-to-all-start.1 = ((bf16[8,32,1024]{2,1,0:T(8,128)(2,1)}), bf16[8,32,1024]{2,1,0:T(8,128)(2,1)S(1)}, u32[]{:S(2)}, u32[]{:S(2)}) async-start(bf16[8,32,1024]{2,1,0:T(8,128)(2,1)} %broadcast_in_dim.7), calls=%async_computation.1 | async-start | bytes 1048576 | tf_op jit(solution)/shard_map/all_to_all | solution.py:147
  65.0 18.5 %copy-start.2 = (s32[4]{0:T(128)S(1)}, s32[4]{0:T(128)}, u32[]{:S(2)}) copy-start(s32[4]{0:T(128)} %constant.117.clone) | copy-start | bytes 52
  65.0 5.7 %collective-permute-start.11 = (bf16[512,256]{1,0:T(8,128)(2,1)S(1)}, bf16[512,256]{1,0:T(8,128)(2,1)S(1)}, u32[]{:S(2)}, u32[]{:S(2)}) collective-permute-start(bf16[512,256]{1,0:T(8,128)(2,1)S(1)} %pad_maximum_fusion.1.refs_2_.refs_4_), channel_id=1, source_target_pairs={{0,1},{1,0},{2,3},{3,2},{4,5},{5,4},{6,7},{7,6},{8,9},{9,8},{10,11... | collective-permute-start | bytes 786440 | tf_op jit(solution)/shard_map/ppermute | solution.py:111
  65.0 10.2 %collective-permute-start.12 = (bf16[512,256]{1,0:T(8,128)(2,1)S(1)}, bf16[512,256]{1,0:T(8,128)(2,1)S(1)}, u32[]{:S(2)}, u32[]{:S(2)}) collective-permute-start(bf16[512,256]{1,0:T(8,128)(2,1)S(1)} %collective-permute-done.8.refs_3_), channel_id=1, source_target_pairs={{0,1},{1,0},{2,3},{3,2},{4,5},{5,4},{6,7},{7,6},{8,9},{9,8},{10,11... | collective-permute-start | bytes 786440 | tf_op jit(solution)/shard_map/ppermute | solution.py:111
  66.5 8.6 %collective-permute-start.13 = (bf16[512,256]{1,0:T(8,128)(2,1)S(1)}, bf16[512,256]{1,0:T(8,128)(2,1)S(1)}, u32[]{:S(2)}, u32[]{:S(2)}) collective-permute-start(bf16[512,256]{1,0:T(8,128)(2,1)S(1)} %collective-permute-done.9.refs_4_), channel_id=1, source_target_pairs={{0,1},{1,0},{2,3},{3,2},{4,5},{5,4},{6,7},{7,6},{8,9},{9,8},{10,11... | collective-permute-start | bytes 786440 | tf_op jit(solution)/shard_map/ppermute | solution.py:111
  70.7 4.5 %collective-permute-start.14 = (bf16[512,256]{1,0:T(8,128)(2,1)S(1)}, bf16[512,256]{1,0:T(8,128)(2,1)S(1)}, u32[]{:S(2)}, u32[]{:S(2)}) collective-permute-start(bf16[512,256]{1,0:T(8,128)(2,1)S(1)} %collective-permute-done.10.refs_5_), channel_id=1, source_target_pairs={{0,1},{1,0},{2,3},{3,2},{4,5},{5,4},{6,7},{7,6},{8,9},{9,8},{10,11... | collective-permute-start | bytes 786440 | tf_op jit(solution)/shard_map/ppermute | solution.py:111
  70.7 15.9 %collective-permute-start.16 = (bf16[1024,256]{1,0:T(8,128)(2,1)S(1)}, bf16[1024,256]{1,0:T(8,128)(2,1)}, u32[]{:S(2)}, u32[]{:S(2)}) collective-permute-start(bf16[1024,256]{1,0:T(8,128)(2,1)S(1)} %pad_maximum_fusion.refs_1_.refs_5_), channel_id=1, source_target_pairs={{0,1},{1,0},{2,3},{3,2},{4,5},{5,4},{6,7},{7,6},{8,9},{9,8},{10,11... | collective-permute-start | bytes 1572872 | tf_op jit(solution)/shard_map/ppermute | solution.py:111
  71.2 19.6 %collective-permute-start.17 = (bf16[1024,256]{1,0:T(8,128)(2,1)}, bf16[1024,256]{1,0:T(8,128)(2,1)}, u32[]{:S(2)}, u32[]{:S(2)}) collective-permute-start(bf16[1024,256]{1,0:T(8,128)(2,1)} %collective-permute-done.15.refs_6_), channel_id=1, source_target_pairs={{0,1},{1,0},{2,3},{3,2},{4,5},{5,4},{6,7},{7,6},{8,9},{9,8},{10,11... | collective-permute-start | bytes 1572872 | tf_op jit(solution)/shard_map/ppermute | solution.py:111
  78.2 12.6 %all-to-all-start.2 = ((bf16[16,8,1152]{2,1,0:T(8,128)(2,1)}), bf16[16,8,1152]{2,1,0:T(8,128)(2,1)S(1)}, u32[]{:S(2)}, u32[]{:S(2)}) async-start(bf16[16,8,1152]{2,1,0:T(8,128)(2,1)} %get-tuple-element.44), calls=%async_computation.2 | async-start | bytes 589824 | tf_op jit(solution)/shard_map/all_to_all | solution.py:147
  90.8 25.2 %copy-start = (bf16[16,8,1152]{2,1,0:T(8,128)(2,1)}, bf16[16,8,1152]{2,1,0:T(8,128)(2,1)S(1)}, u32[]{:S(2)}) copy-start(bf16[16,8,1152]{2,1,0:T(8,128)(2,1)S(1)} %all-to-all-done.2.refs_1_.refs_5_) | copy-start | bytes 884740
  116.0 11.1 %collective-permute-start.18 = (bf16[96,512]{1,0:T(8,128)(2,1)S(1)}, bf16[96,512]{1,0:T(8,128)(2,1)S(1)}, u32[]{:S(2)}, u32[]{:S(2)}) collective-permute-start(bf16[96,512]{1,0:T(8,128)(2,1)S(1)} %get-tuple-element.51), channel_id=1, source_target_pairs={{0,16},{16,32},{32,48},{48,64},{64,80},{80,96},{96,112},{1,17},{17... | collective-permute-start | bytes 294920 | tf_op jit(solution)/shard_map/ppermute | solution.py:118
  118.5 8.6 %collective-permute-start.19 = (bf16[96,512]{1,0:T(8,128)(2,1)S(1)}, bf16[96,512]{1,0:T(8,128)(2,1)S(1)}, u32[]{:S(2)}, u32[]{:S(2)}) collective-permute-start(bf16[96,512]{1,0:T(8,128)(2,1)S(1)} %get-tuple-element.52), channel_id=1, source_target_pairs={{16,0},{32,16},{48,32},{64,48},{80,64},{96,80},{112,96},{17,1},{33... | collective-permute-start | bytes 294920 | tf_op jit(solution)/shard_map/ppermute | solution.py:118
  127.3 13.7 %collective-permute-start.20 = (bf16[80,512]{1,0:T(8,128)(2,1)S(1)}, bf16[80,512]{1,0:T(8,128)(2,1)S(1)}, u32[]{:S(2)}, u32[]{:S(2)}) collective-permute-start(bf16[80,512]{1,0:T(8,128)(2,1)S(1)} %get-tuple-element.68), channel_id=1, source_target_pairs={{0,1},{1,2},{2,3},{3,4},{4,5},{5,6},{6,7},{7,8},{8,9},{9,10},{10,1... | collective-permute-start | bytes 245768 | tf_op jit(solution)/shard_map/ppermute | solution.py:118
  129.2 11.8 %collective-permute-start.21 = (bf16[80,512]{1,0:T(8,128)(2,1)S(1)}, bf16[80,512]{1,0:T(8,128)(2,1)S(1)}, u32[]{:S(2)}, u32[]{:S(2)}) collective-permute-start(bf16[80,512]{1,0:T(8,128)(2,1)S(1)} %get-tuple-element.69), channel_id=1, source_target_pairs={{1,0},{2,1},{3,2},{4,3},{5,4},{6,5},{7,6},{8,7},{9,8},{10,9},{11,1... | collective-permute-start | bytes 245768 | tf_op jit(solution)/shard_map/ppermute | solution.py:118

commit v3 on v1

--- a/solution.py
+++ b/solution.py
@@ -391,12 +391,12 @@
         out = dot(weight, v_out[:, to])
         norm = out[:, DELTA_LANE : DELTA_LANE + 1]
         q_out[:, to] = at_lanes(q, lane, LSE_LANE, top + jnp.log(norm)).astype(bf16)
-        out = jnp.where(channel, out / norm, 0.0)
-        a0_out[:, at] = out.astype(bf16)
-        outs.append(out)
+        outs.append(out / norm)
+    a0 = as_pairs(outs)
+    a0_out[...] = a0
     for result in (q_one, q_two, k_one, k_two, v_one, v_two, q_halo_out, a0_out):
         result.send()
-    y = (x + dot(as_pairs(outs), w_out_ref[...])).astype(bf16)
+    y = (x + dot(a0, w_out_ref[...])).astype(bf16)
     quarter = own // 4
     m1 = dot(y[:quarter], one_ref[:C0])
     for part in range(1, 4):
@@ -528,12 +528,13 @@
     dy_out[...] = dy
     dy_out.send()
     da0 = dot_last(dy, w_out_ref[...]).astype(bf16).astype(f32)
+    a0 = a0_ref[...].astype(f32)
     lane = lax.broadcasted_iota(jnp.int32, (1, LANES), 1)
     is_lse = (lane == LSE_LANE) | (lane == LSE_LANE + 1)
     for h in range(NA_HEADS):
         at = head_lanes(h)
         mine = jnp.where(lane < NA_DIM, head_of(da0, h), 0.0)
-        delta = jnp.sum(mine * a0_ref[:, at].astype(f32), -1, keepdims=True)
+        delta = jnp.sum(mine * head_of(a0, h), -1, keepdims=True)
         q_ref = q_two if h // 2 else q_one
         mine = jnp.where(is_lse, q_ref[:, head_lanes(h % 2)].astype(f32), mine)
         dout_out[:, at] = at_lanes(mine, lane, DELTA_LANE, delta).astype(bf16)
@@ -693,7 +694,7 @@
             ((own + padded, WIDE // 2), bf16),
             ((own + padded, WIDE // 2), bf16),
             ((padded, WIDE), bf16),
-            ((own, WIDE), bf16),
+            ((own, C0), bf16),
         ],
         (
             flat,

time: 147 us -> 148 us (level)
  no operation moved by 1% of the time
where the time goes in v3:
time: 148 us; the launch traced here: 147 us
  starting transfers between devices  49 us (33%)
  Pallas kernels  43.5 us (29%)
  blocking collectives  25.3 us (17%)
  waiting for transfers between devices  20.5 us (14%)
  local copies, waits for them, and re-layouts  3.42 us (2%)
  matrix products  2.34 us (2%)
  other arithmetic  1.51 us (1%)
    pallas_call x10, Pallas kernels, call(): pl.pallas_call(body, out_shape=[pltpu.HBM(*out) if i in out_manual else j...  43.5 us
    all_to_all x2, blocking collectives, all_to_all(): return lax.all_to_all(array, axis, split_axis=0, concat_axis=0, tiled=True)  25.3 us
    ppermute x4, starting transfers between devices, neighbours(): lax.ppermute(to_previous, axis, down)  18.1 us
    ppermute x14, starting transfers between devices, shifted(): return lax.ppermute(array, axis, [(i, move(i)) for i in range(count)])  11.2 us
    ppermute x14, waiting for transfers between devices, shifted(): return lax.ppermute(array, axis, [(i, move(i)) for i in range(count)])  10.6 us
    all_to_all x2, starting transfers between devices, all_to_all(): return lax.all_to_all(array, axis, split_axis=0, concat_axis=0, tiled=True)  9.92 us
    ppermute x4, starting transfers between devices, neighbours(): lax.ppermute(to_next, axis, up)  9.76 us
    all_to_all x2, waiting for transfers between devices, all_to_all(): return lax.all_to_all(array, axis, split_axis=0, concat_axis=0, tiled=True)  7.91 us
  transfers between devices with their start and end apart: 24, of which 10 were waited for; matrix products, arithmetic and copies ran while one was open for 4% of the time, Pallas kernels for 11%

profile of v3, /device:TPU:34, one launch (start us, length us, event | category | flops | bytes accessed | tf_op | source)
XLA Modules:
  0.0 146.8 jit_solution(9346609508417207450)
XLA Ops:
  1.5 3.4 %collective-permute-start = (bf16[96,256]{1,0:T(8,128)(2,1)S(1)}, bf16[96,256]{1,0:T(8,128)(2,1)S(1)}, u32[]{:S(2)}, u32[]{:S(2)}) collective-permute-start(bf16[96,256]{1,0:T(8,128)(2,1)S(1)} %bitcast.22), channel_id=1, source_target_pairs={{0,16},{16,32},{32,48},{48,64},{64,80},{80,96},{96,112},{1,17},{17... | collective-permute-start | bytes 147464 | tf_op jit(solution)/shard_map/ppermute | solution.py:118
  5.0 2.4 %collective-permute-start.1 = (bf16[96,256]{1,0:T(8,128)(2,1)S(1)}, bf16[96,256]{1,0:T(8,128)(2,1)S(1)}, u32[]{:S(2)}, u32[]{:S(2)}) collective-permute-start(bf16[96,256]{1,0:T(8,128)(2,1)S(1)} %bitcast.21), channel_id=1, source_target_pairs={{16,0},{32,16},{48,32},{64,48},{80,64},{96,80},{112,96},{17,1},{33... | collective-permute-start | bytes 147464 | tf_op jit(solution)/shard_map/ppermute | solution.py:118
  8.3 2.3 %convolution_convert_fusion.refs_14_ = bf16[32,1024]{1,0:T(8,128)(2,1)S(1)} fusion(bf16[1024,1024]{1,0:T(8,128)(2,1)} %refs_6_.3, bf16[4,8,1024]{2,1,0:T(8,128)(2,1)} %param.25), kind=kOutput, calls=%fused_computation.1 | convolution fusion | flops 67141632 | bytes 2228224 | tf_op jit(solution)/shard_map/dot_general | solution.py:37
  10.8 1.1 collective-permute-done.1.refs_2_.refs_4_
  12.1 1.9 %collective-permute-start.2 = (bf16[80,256]{1,0:T(8,128)(2,1)S(1)}, bf16[80,256]{1,0:T(8,128)(2,1)S(1)}, u32[]{:S(2)}, u32[]{:S(2)}) collective-permute-start(bf16[80,256]{1,0:T(8,128)(2,1)S(1)} %get-tuple-element.37), channel_id=1, source_target_pairs={{0,1},{1,2},{2,3},{3,4},{4,5},{5,6},{6,7},{7,8},{8,9},{9,10},{10,1... | collective-permute-start | bytes 122888 | tf_op jit(solution)/shard_map/ppermute | solution.py:118
  14.0 6.0 %collective-permute-start.3 = (bf16[80,256]{1,0:T(8,128)(2,1)S(1)}, bf16[80,256]{1,0:T(8,128)(2,1)S(1)}, u32[]{:S(2)}, u32[]{:S(2)}) collective-permute-start(bf16[80,256]{1,0:T(8,128)(2,1)S(1)} %get-tuple-element.38), channel_id=1, source_target_pairs={{1,0},{2,1},{3,2},{4,3},{5,4},{6,5},{7,6},{8,7},{9,8},{10,9},{11,1... | collective-permute-start | bytes 122888 | tf_op jit(solution)/shard_map/ppermute | solution.py:118
  21.7 9.5 %shard_map.194 = (bf16[8,32,512]{2,1,0:T(8,128)(2,1)S(1)}, bf16[32,1024]{1,0:T(8,128)(2,1)}, bf16[512,256]{1,0:T(8,128)(2,1)}, bf16[512,256]{1,0:T(8,128)(2,1)},...) custom-call(bf16[512,256]{1,0:T(8,128)(2,1)} %bitcast.17, ...), custom_call_target="tpu_custom_call" | custom-call | tf_op jit(solution)/shard_map/pallas_call | solution.py:263
  31.2 12.8 %all_to_all.20 = bf16[8,32,512]{2,1,0:T(8,128)(2,1)S(1)} all-to-all(bf16[8,32,512]{2,1,0:T(8,128)(2,1)S(1)} %get-tuple-element.39), channel_id=1, replica_groups=mesh['row'=8,'col'=16] {'row'}, dimensions={0} | all-to-all | bytes 524288 | tf_op jit(solution)/shard_map/all_to_all | solution.py:147
  44.0 3.0 %collective-permute-start.7 = (bf16[256,256]{1,0:T(8,128)(2,1)S(1)}, bf16[256,256]{1,0:T(8,128)(2,1)S(1)}, u32[]{:S(2)}, u32[]{:S(2)}) collective-permute-start(bf16[256,256]{1,0:T(8,128)(2,1)S(1)} %get-tuple-element.71), channel_id=1, source_target_pairs={{0,8},{1,9},{2,10},{3,11},{4,12},{5,13},{6,14},{7,15},{8,0},{9,1},... | collective-permute-start | bytes 393224 | tf_op jit(solution)/shard_map/ppermute | solution.py:111
  48.0 1.0 collective-permute-start.5
  49.5 2.4 %collective-permute-done.7 = bf16[256,256]{1,0:T(8,128)(2,1)S(1)} collective-permute-done((bf16[256,256]{1,0:T(8,128)(2,1)S(1)}, bf16[256,256]{1,0:T(8,128)(2,1)S(1)}, u32[]{:S(2)}, u32[]{:S(2)}) %collective-permute-start.7) | collective-permute-done | bytes 131104 | tf_op jit(solution)/shard_map/ppermute | solution.py:111
  51.9 2.0 %collective-permute-done.6 = bf16[256,256]{1,0:T(8,128)(2,1)S(1)} collective-permute-done((bf16[256,256]{1,0:T(8,128)(2,1)S(1)}, bf16[256,256]{1,0:T(8,128)(2,1)S(1)}, u32[]{:S(2)}, u32[]{:S(2)}) %collective-permute-start.6) | collective-permute-done | bytes 131104 | tf_op jit(solution)/shard_map/ppermute | solution.py:111
  55.6 1.7 %collective-permute-start.8 = (bf16[512,256]{1,0:T(8,128)(2,1)S(1)}, bf16[512,256]{1,0:T(8,128)(2,1)S(1)}, u32[]{:S(2)}, u32[]{:S(2)}) collective-permute-start(bf16[512,256]{1,0:T(8,128)(2,1)S(1)} %pad_maximum_fusion.1.refs_2_.refs_4_), channel_id=1, source_target_pairs={{0,4},{1,5},{2,6},{3,7},{4,8},{5,9},{6,10},{7,11},{8,12},{9,13},{1... | collective-permute-start | bytes 786440 | tf_op jit(solution)/shard_map/ppermute | solution.py:111
  57.7 1.8 %collective-permute-start.10 = (bf16[512,256]{1,0:T(8,128)(2,1)S(1)}, bf16[512,256]{1,0:T(8,128)(2,1)S(1)}, u32[]{:S(2)}, u32[]{:S(2)}) collective-permute-start(bf16[512,256]{1,0:T(8,128)(2,1)S(1)} %pad_maximum_fusion.1.refs_2_.refs_4_), channel_id=1, source_target_pairs={{0,8},{1,9},{2,10},{3,11},{4,12},{5,13},{6,14},{7,15},{8,0},{9,1},... | collective-permute-start | bytes 786440 | tf_op jit(solution)/shard_map/ppermute | solution.py:111
  60.3 4.7 %all-to-all-start.1 = ((bf16[8,32,1024]{2,1,0:T(8,128)(2,1)}), bf16[8,32,1024]{2,1,0:T(8,128)(2,1)S(1)}, u32[]{:S(2)}, u32[]{:S(2)}) async-start(bf16[8,32,1024]{2,1,0:T(8,128)(2,1)} %broadcast_in_dim.7), calls=%async_computation.1 | async-start | bytes 1048576 | tf_op jit(solution)/shard_map/all_to_all | solution.py:147
  65.5 1.0 collective-permute-done.9.refs_4_
  66.5 4.1 %collective-permute-done.10.refs_5_ = bf16[512,256]{1,0:T(8,128)(2,1)S(1)} collective-permute-done((bf16[512,256]{1,0:T(8,128)(2,1)S(1)}, bf16[512,256]{1,0:T(8,128)(2,1)S(1)}, u32[]{:S(2)}, u32[]{:S(2)}) %collective-permute-start.10) | collective-permute-done | bytes 262176 | tf_op jit(solution)/shard_map/ppermute | solution.py:111
  71.5 3.7 %all-to-all-done.1 = bf16[8,32,1024]{2,1,0:T(8,128)(2,1)S(1)} async-done(((bf16[8,32,1024]{2,1,0:T(8,128)(2,1)}), bf16[8,32,1024]{2,1,0:T(8,128)(2,1)S(1)}, u32[]{:S(2)}, u32[]{:S(2)}) %all-to-all-start.1) | async-done | bytes 524320 | tf_op jit(solution)/shard_map/all_to_all | solution.py:147
  75.2 3.1 %shard_map.195 = (bf16[256,128]{1,0:T(8,128)(2,1)S(1)}, f32[256,128]{1,0:T(8,128)S(1)}, bf16[16,8,1152]{2,1,0:T(8,128)(2,1)}) custom-call(bf16[256,1024]{1,0:T(8,128)(2,1)S(1)} %bitcast.14, bf16[1024,256]{1,0:T(8,128)(2,1)S(1)} %pad_maximum_fusion.refs_1_.refs_5_, bf16[512,256]{1,0:T(8,128)(2,1)S(1)} %pad_maximum_fusion.1.refs_2_.refs_4_, ...), custom_call_target="tpu_custom_call" | custom-call | tf_op jit(solution)/shard_map/pallas_call | solution.py:263
  78.2 5.2 %all-to-all-start.2 = ((bf16[16,8,1152]{2,1,0:T(8,128)(2,1)}), bf16[16,8,1152]{2,1,0:T(8,128)(2,1)S(1)}, u32[]{:S(2)}, u32[]{:S(2)}) async-start(bf16[16,8,1152]{2,1,0:T(8,128)(2,1)} %get-tuple-element.42), calls=%async_computation.2 | async-start | bytes 589824 | tf_op jit(solution)/shard_map/all_to_all | solution.py:147
  84.2 2.4 %shard_map.196.refs_2_ = bf16[256,128]{1,0:T(8,128)(2,1)S(1)} custom-call(f32[256,128]{1,0:T(8,128)S(1)} %get-tuple-element.43.refs_0_, bf16[1024,256]{1,0:T(8,128)(2,1)S(1)} %pad_maximum_fusion.refs_1_.refs_5_, bf16[512,256]{1,0:T(8,128)(2,1)S(1)} %pad_maximum_fusion.1.refs_2_.refs_4_, bf16[512,256]{1,0:T(8,128)(2,1)S(1)} %collective-permute-done.8.refs_3_, ...), custom_call_target="tpu_custom_call" | custom-call | tf_op jit(solution)/shard_map/pallas_call | solution.py:263
  86.6 4.2 %all-to-all-done.2.refs_1_ = bf16[16,8,1152]{2,1,0:T(8,128)(2,1)S(1)} async-done(((bf16[16,8,1152]{2,1,0:T(8,128)(2,1)}), bf16[16,8,1152]{2,1,0:T(8,128)(2,1)S(1)}, u32[]{:S(2)}, u32[]{:S(2)}) %all-to-all-start.2) | async-done | bytes 294944 | tf_op jit(solution)/shard_map/all_to_all | solution.py:147
  90.8 4.2 %shard_map.197 = bf16[256,512]{1,0:T(8,128)(2,1)S(1)} custom-call(s32[16]{0:T(128)S(1)} %fusion.5.refs_0_, bf16[16,8,1152]{2,1,0:T(8,128)(2,1)S(1)} %all-to-all-done.2.refs_1_, bf16[256,128]{1,0:T(8,128)(2,1)S(1)} %shard_map.196.refs_2_, bf16[256,128]{1,0:T(8,128)(2,1)S(1)} %get-tuple-element.44.refs_3_, ...), custom_call_target="tpu_custom_call" | custom-call | tf_op jit(solution)/shard_map/pallas_call | solution.py:263
  95.0 12.5 %all_to_all.21.refs_0_.refs_5_ = bf16[8,32,512]{2,1,0:T(8,128)(2,1)S(1)} all-to-all(bf16[8,32,512]{2,1,0:T(8,128)(2,1)S(1)} %bitcast.15), channel_id=1, replica_groups=mesh['row'=8,'col'=16] {'row'}, dimensions={0} | all-to-all | bytes 524288 | tf_op jit(solution)/shard_map/all_to_all | solution.py:147
  107.6 8.3 %shard_map.198 = (bf16[512,512]{1,0:T(8,128)(2,1)S(1)}, bf16[512,256]{1,0:T(8,128)(2,1)}, bf16[96,512]{1,0:T(8,128)(2,1)S(1)}, bf16[96,512]{1,0:T(8,128)(2,1)S(1...) custom-call(bf16[8,32,512]{2,1,0:T(8,128)(2,1)S(1)} %all_to_all.21.refs_0_.refs_5_, ...), custom_call_target="tpu_custom_call" | custom-call | tf_op jit(solution)/shard_map/pallas_call | solution.py:263
  115.9 2.5 %collective-permute-start.18 = (bf16[96,512]{1,0:T(8,128)(2,1)S(1)}, bf16[96,512]{1,0:T(8,128)(2,1)S(1)}, u32[]{:S(2)}, u32[]{:S(2)}) collective-permute-start(bf16[96,512]{1,0:T(8,128)(2,1)S(1)} %get-tuple-element.49), channel_id=1, source_target_pairs={{0,16},{16,32},{32,48},{48,64},{64,80},{80,96},{96,112},{1,17},{17... | collective-permute-start | bytes 294920 | tf_op jit(solution)/shard_map/ppermute | solution.py:118
  118.4 3.6 %collective-permute-start.19 = (bf16[96,512]{1,0:T(8,128)(2,1)S(1)}, bf16[96,512]{1,0:T(8,128)(2,1)S(1)}, u32[]{:S(2)}, u32[]{:S(2)}) collective-permute-start(bf16[96,512]{1,0:T(8,128)(2,1)S(1)} %get-tuple-element.50), channel_id=1, source_target_pairs={{16,0},{32,16},{48,32},{64,48},{80,64},{96,80},{112,96},{17,1},{33... | collective-permute-start | bytes 294920 | tf_op jit(solution)/shard_map/ppermute | solution.py:118
  122.0 4.3 %shard_map.199.refs_12_ = f32[512,256]{1,0:T(8,128)S(1)} custom-call(bf16[512,256]{1,0:T(8,128)(2,1)} %get-tuple-element.47.refs_8_.refs_0_, bf16[896,256]{1,0:T(8,128)(2,1)} %get-tuple-element.51.refs_1_.refs_2_, bf16[512,512]{1,0:T(8,128)(2,1)S(1)} %get-tuple-element.52.refs_2_, bf16[896,256]{1,0:T(8,128)(2,1)} %get-tuple-element.53.refs_3_, ...), custom_call_target="tpu_custom_call" | custom-call | tf_op jit(solution)/shard_map/pallas_call | solution.py:263
  126.5 1.9 %collective-permute-start.20 = (bf16[80,512]{1,0:T(8,128)(2,1)S(1)}, bf16[80,512]{1,0:T(8,128)(2,1)S(1)}, u32[]{:S(2)}, u32[]{:S(2)}) collective-permute-start(bf16[80,512]{1,0:T(8,128)(2,1)S(1)} %get-tuple-element.65), channel_id=1, source_target_pairs={{0,1},{1,2},{2,3},{3,4},{4,5},{5,6},{6,7},{7,8},{8,9},{9,10},{10,1... | collective-permute-start | bytes 245768 | tf_op jit(solution)/shard_map/ppermute | solution.py:118
  128.4 6.0 %collective-permute-start.21 = (bf16[80,512]{1,0:T(8,128)(2,1)S(1)}, bf16[80,512]{1,0:T(8,128)(2,1)S(1)}, u32[]{:S(2)}, u32[]{:S(2)}) collective-permute-start(bf16[80,512]{1,0:T(8,128)(2,1)S(1)} %get-tuple-element.66), channel_id=1, source_target_pairs={{1,0},{2,1},{3,2},{4,3},{5,4},{6,5},{7,6},{8,7},{9,8},{10,9},{11,1... | collective-permute-start | bytes 245768 | tf_op jit(solution)/shard_map/ppermute | solution.py:118
  135.2 5.7 %shard_map.201 = (f32[512,256]{1,0:T(8,128)S(1)}, bf16[32,1024]{1,0:T(8,128)(2,1)}) custom-call(bf16[512,256]{1,0:T(8,128)(2,1)} %get-tuple-element.60.refs_9_.refs_0_, bf16[896,256]{1,0:T(8,128)(2,1)} %get-tuple-element.61.refs_1_.refs_4_, bf16[512,512]{1,0:T(8,128)(2,1)S(1)} %get-tuple-element.52.refs_2_, ...), custom_call_target="tpu_custom_call" | custom-call | tf_op jit(solution)/shard_map/pallas_call | solution.py:263
  140.9 5.7 %shard_map.202 = bf16[512,256]{1,0:T(8,128)(2,1)} custom-call(bf16[512,128]{1,0:T(8,128)(2,1)} %constant.113.clone.refs_7_.refs_0_, bf16[384,512]{1,0:T(8,128)(2,1)} %get-tuple-element.64.refs_1_, bf16[896,256]{1,0:T(8,128)(2,1)} %get-tuple-element.51.refs_1_.refs_2_, bf16[896,256]{1,0:T(8,128)(2,1)} %get-tuple-element.53.refs_3_, ...), custom_call_target="tpu_custom_call" | custom-call | tf_op jit(solution)/shard_map/pallas_call | solution.py:263
  (57 shorter events, 10.9 us)
Async XLA Ops:
  0.6 10.0 %copy-start.4 = (s32[384]{0:T(512)S(1)}, s32[384]{0:T(512)}, u32[]{:S(2)}) copy-start(s32[384]{0:T(512)} %constant.117.clone) | copy-start | bytes 4612
  0.6 10.0 %copy-start.5 = (s32[384]{0:T(512)S(1)}, s32[384]{0:T(512)}, u32[]{:S(2)}) copy-start(s32[384]{0:T(512)} %constant.116.clone) | copy-start | bytes 4612
  0.7 11.2 %copy-start = (bf16[32,96]{1,0:T(8,128)(2,1)S(1)}, bf16[32,96]{1,0:T(8,128)(2,1)}, u32[]{:S(2)}) copy-start(bf16[32,96]{1,0:T(8,128)(2,1)} %constant.114.clone.refs_0_) | copy-start | bytes 18436
  0.7 19.4 %copy-start.3 = (bf16[384,128]{1,0:T(8,128)(2,1)S(1)}, bf16[384,128]{1,0:T(8,128)(2,1)}, u32[]{:S(2)}) copy-start(bf16[384,128]{1,0:T(8,128)(2,1)} %constant.158) | copy-start | bytes 294916
  1.5 9.2 %collective-permute-start = (bf16[96,256]{1,0:T(8,128)(2,1)S(1)}, bf16[96,256]{1,0:T(8,128)(2,1)S(1)}, u32[]{:S(2)}, u32[]{:S(2)}) collective-permute-start(bf16[96,256]{1,0:T(8,128)(2,1)S(1)} %bitcast.22), channel_id=1, source_target_pairs={{0,16},{16,32},{32,48},{48,64},{64,80},{80,96},{96,112},{1,17},{17... | collective-permute-start | bytes 147464 | tf_op jit(solution)/shard_map/ppermute | solution.py:118
  5.0 6.9 %collective-permute-start.1 = (bf16[96,256]{1,0:T(8,128)(2,1)S(1)}, bf16[96,256]{1,0:T(8,128)(2,1)S(1)}, u32[]{:S(2)}, u32[]{:S(2)}) collective-permute-start(bf16[96,256]{1,0:T(8,128)(2,1)S(1)} %bitcast.21), channel_id=1, source_target_pairs={{16,0},{32,16},{48,32},{64,48},{80,64},{96,80},{112,96},{17,1},{33... | collective-permute-start | bytes 147464 | tf_op jit(solution)/shard_map/ppermute | solution.py:118
  12.1 8.7 %collective-permute-start.2 = (bf16[80,256]{1,0:T(8,128)(2,1)S(1)}, bf16[80,256]{1,0:T(8,128)(2,1)S(1)}, u32[]{:S(2)}, u32[]{:S(2)}) collective-permute-start(bf16[80,256]{1,0:T(8,128)(2,1)S(1)} %get-tuple-element.37), channel_id=1, source_target_pairs={{0,1},{1,2},{2,3},{3,4},{4,5},{5,6},{6,7},{7,8},{8,9},{9,10},{10,1... | collective-permute-start | bytes 122888 | tf_op jit(solution)/shard_map/ppermute | solution.py:118
  14.0 7.7 %collective-permute-start.3 = (bf16[80,256]{1,0:T(8,128)(2,1)S(1)}, bf16[80,256]{1,0:T(8,128)(2,1)S(1)}, u32[]{:S(2)}, u32[]{:S(2)}) collective-permute-start(bf16[80,256]{1,0:T(8,128)(2,1)S(1)} %get-tuple-element.38), channel_id=1, source_target_pairs={{1,0},{2,1},{3,2},{4,3},{5,4},{6,5},{7,6},{8,7},{9,8},{10,9},{11,1... | collective-permute-start | bytes 122888 | tf_op jit(solution)/shard_map/ppermute | solution.py:118
  31.2 28.3 %copy-start.2 = (bf16[4,8,1024]{2,1,0:T(8,128)(2,1)S(1)}, bf16[4,8,1024]{2,1,0:T(8,128)(2,1)}, u32[]{:S(2)}) copy-start(bf16[4,8,1024]{2,1,0:T(8,128)(2,1)} %param.25) | copy-start | bytes 196612
  44.0 7.9 %collective-permute-start.7 = (bf16[256,256]{1,0:T(8,128)(2,1)S(1)}, bf16[256,256]{1,0:T(8,128)(2,1)S(1)}, u32[]{:S(2)}, u32[]{:S(2)}) collective-permute-start(bf16[256,256]{1,0:T(8,128)(2,1)S(1)} %get-tuple-element.71), channel_id=1, source_target_pairs={{0,8},{1,9},{2,10},{3,11},{4,12},{5,13},{6,14},{7,15},{8,0},{9,1},... | collective-permute-start | bytes 393224 | tf_op jit(solution)/shard_map/ppermute | solution.py:111
  47.0 6.9 %collective-permute-start.6 = (bf16[256,256]{1,0:T(8,128)(2,1)S(1)}, bf16[256,256]{1,0:T(8,128)(2,1)S(1)}, u32[]{:S(2)}, u32[]{:S(2)}) collective-permute-start(bf16[256,256]{1,0:T(8,128)(2,1)S(1)} %get-tuple-element.71), channel_id=1, source_target_pairs={{0,12},{1,13},{2,14},{3,15},{4,0},{5,1},{6,2},{7,3},{8,4},{9,5},{1... | collective-permute-start | bytes 393224 | tf_op jit(solution)/shard_map/ppermute | solution.py:111
  48.0 6.3 %collective-permute-start.5 = (bf16[256,256]{1,0:T(8,128)(2,1)S(1)}, bf16[256,256]{1,0:T(8,128)(2,1)S(1)}, u32[]{:S(2)}, u32[]{:S(2)}) collective-permute-start(bf16[256,256]{1,0:T(8,128)(2,1)S(1)} %get-tuple-element.71), channel_id=1, source_target_pairs={{0,4},{1,5},{2,6},{3,7},{4,8},{5,9},{6,10},{7,11},{8,12},{9,13},{1... | collective-permute-start | bytes 393224 | tf_op jit(solution)/shard_map/ppermute | solution.py:111
  49.1 6.5 %collective-permute-start.4 = (bf16[256,256]{1,0:T(8,128)(2,1)S(1)}, bf16[256,256]{1,0:T(8,128)(2,1)S(1)}, u32[]{:S(2)}, u32[]{:S(2)}) collective-permute-start(bf16[256,256]{1,0:T(8,128)(2,1)S(1)} %get-tuple-element.72), channel_id=1, source_target_pairs={{0,2},{1,3},{2,0},{3,1},{4,6},{5,7},{6,4},{7,5},{8,10},{9,11},{10,... | collective-permute-start | bytes 393224 | tf_op jit(solution)/shard_map/ppermute | solution.py:111
  54.4 16.8 %collective-permute-start.15 = (bf16[1024,256]{1,0:T(8,128)(2,1)S(1)}, bf16[1024,256]{1,0:T(8,128)(2,1)}, u32[]{:S(2)}, u32[]{:S(2)}) collective-permute-start(bf16[1024,256]{1,0:T(8,128)(2,1)S(1)} %pad_maximum_fusion.refs_1_.refs_5_), channel_id=1, source_target_pairs={{0,2},{1,3},{2,0},{3,1},{4,6},{5,7},{6,4},{7,5},{8,10},{9,11},{10,... | collective-permute-start | bytes 1572872 | tf_op jit(solution)/shard_map/ppermute | solution.py:111
  55.6 9.4 %collective-permute-start.8 = (bf16[512,256]{1,0:T(8,128)(2,1)S(1)}, bf16[512,256]{1,0:T(8,128)(2,1)S(1)}, u32[]{:S(2)}, u32[]{:S(2)}) collective-permute-start(bf16[512,256]{1,0:T(8,128)(2,1)S(1)} %pad_maximum_fusion.1.refs_2_.refs_4_), channel_id=1, source_target_pairs={{0,4},{1,5},{2,6},{3,7},{4,8},{5,9},{6,10},{7,11},{8,12},{9,13},{1... | collective-permute-start | bytes 786440 | tf_op jit(solution)/shard_map/ppermute | solution.py:111
  57.3 9.2 %collective-permute-start.9 = (bf16[512,256]{1,0:T(8,128)(2,1)S(1)}, bf16[512,256]{1,0:T(8,128)(2,1)S(1)}, u32[]{:S(2)}, u32[]{:S(2)}) collective-permute-start(bf16[512,256]{1,0:T(8,128)(2,1)S(1)} %pad_maximum_fusion.1.refs_2_.refs_4_), channel_id=1, source_target_pairs={{0,12},{1,13},{2,14},{3,15},{4,0},{5,1},{6,2},{7,3},{8,4},{9,5},{1... | collective-permute-start | bytes 786440 | tf_op jit(solution)/shard_map/ppermute | solution.py:111
  57.7 13.0 %collective-permute-start.10 = (bf16[512,256]{1,0:T(8,128)(2,1)S(1)}, bf16[512,256]{1,0:T(8,128)(2,1)S(1)}, u32[]{:S(2)}, u32[]{:S(2)}) collective-permute-start(bf16[512,256]{1,0:T(8,128)(2,1)S(1)} %pad_maximum_fusion.1.refs_2_.refs_4_), channel_id=1, source_target_pairs={{0,8},{1,9},{2,10},{3,11},{4,12},{5,13},{6,14},{7,15},{8,0},{9,1},... | collective-permute-start | bytes 786440 | tf_op jit(solution)/shard_map/ppermute | solution.py:111
  60.3 14.9 %all-to-all-start.1 = ((bf16[8,32,1024]{2,1,0:T(8,128)(2,1)}), bf16[8,32,1024]{2,1,0:T(8,128)(2,1)S(1)}, u32[]{:S(2)}, u32[]{:S(2)}) async-start(bf16[8,32,1024]{2,1,0:T(8,128)(2,1)} %broadcast_in_dim.7), calls=%async_computation.1 | async-start | bytes 1048576 | tf_op jit(solution)/shard_map/all_to_all | solution.py:147
  65.0 18.5 %copy-start.1 = (s32[4]{0:T(128)S(1)}, s32[4]{0:T(128)}, u32[]{:S(2)}) copy-start(s32[4]{0:T(128)} %constant.119.clone) | copy-start | bytes 52
  65.0 5.7 %collective-permute-start.11 = (bf16[512,256]{1,0:T(8,128)(2,1)S(1)}, bf16[512,256]{1,0:T(8,128)(2,1)S(1)}, u32[]{:S(2)}, u32[]{:S(2)}) collective-permute-start(bf16[512,256]{1,0:T(8,128)(2,1)S(1)} %pad_maximum_fusion.1.refs_2_.refs_4_), channel_id=1, source_target_pairs={{0,1},{1,0},{2,3},{3,2},{4,5},{5,4},{6,7},{7,6},{8,9},{9,8},{10,11... | collective-permute-start | bytes 786440 | tf_op jit(solution)/shard_map/ppermute | solution.py:111
  65.0 10.2 %collective-permute-start.12 = (bf16[512,256]{1,0:T(8,128)(2,1)S(1)}, bf16[512,256]{1,0:T(8,128)(2,1)S(1)}, u32[]{:S(2)}, u32[]{:S(2)}) collective-permute-start(bf16[512,256]{1,0:T(8,128)(2,1)S(1)} %collective-permute-done.8.refs_3_), channel_id=1, source_target_pairs={{0,1},{1,0},{2,3},{3,2},{4,5},{5,4},{6,7},{7,6},{8,9},{9,8},{10,11... | collective-permute-start | bytes 786440 | tf_op jit(solution)/shard_map/ppermute | solution.py:111
  66.5 8.6 %collective-permute-start.13 = (bf16[512,256]{1,0:T(8,128)(2,1)S(1)}, bf16[512,256]{1,0:T(8,128)(2,1)S(1)}, u32[]{:S(2)}, u32[]{:S(2)}) collective-permute-start(bf16[512,256]{1,0:T(8,128)(2,1)S(1)} %collective-permute-done.9.refs_4_), channel_id=1, source_target_pairs={{0,1},{1,0},{2,3},{3,2},{4,5},{5,4},{6,7},{7,6},{8,9},{9,8},{10,11... | collective-permute-start | bytes 786440 | tf_op jit(solution)/shard_map/ppermute | solution.py:111
  70.7 4.5 %collective-permute-start.14 = (bf16[512,256]{1,0:T(8,128)(2,1)S(1)}, bf16[512,256]{1,0:T(8,128)(2,1)S(1)}, u32[]{:S(2)}, u32[]{:S(2)}) collective-permute-start(bf16[512,256]{1,0:T(8,128)(2,1)S(1)} %collective-permute-done.10.refs_5_), channel_id=1, source_target_pairs={{0,1},{1,0},{2,3},{3,2},{4,5},{5,4},{6,7},{7,6},{8,9},{9,8},{10,11... | collective-permute-start | bytes 786440 | tf_op jit(solution)/shard_map/ppermute | solution.py:111
  70.7 15.9 %collective-permute-start.16 = (bf16[1024,256]{1,0:T(8,128)(2,1)S(1)}, bf16[1024,256]{1,0:T(8,128)(2,1)}, u32[]{:S(2)}, u32[]{:S(2)}) collective-permute-start(bf16[1024,256]{1,0:T(8,128)(2,1)S(1)} %pad_maximum_fusion.refs_1_.refs_5_), channel_id=1, source_target_pairs={{0,1},{1,0},{2,3},{3,2},{4,5},{5,4},{6,7},{7,6},{8,9},{9,8},{10,11... | collective-permute-start | bytes 1572872 | tf_op jit(solution)/shard_map/ppermute | solution.py:111
  71.2 19.6 %collective-permute-start.17 = (bf16[1024,256]{1,0:T(8,128)(2,1)}, bf16[1024,256]{1,0:T(8,128)(2,1)}, u32[]{:S(2)}, u32[]{:S(2)}) collective-permute-start(bf16[1024,256]{1,0:T(8,128)(2,1)} %collective-permute-done.15.refs_6_), channel_id=1, source_target_pairs={{0,1},{1,0},{2,3},{3,2},{4,5},{5,4},{6,7},{7,6},{8,9},{9,8},{10,11... | collective-permute-start | bytes 1572872 | tf_op jit(solution)/shard_map/ppermute | solution.py:111
  78.2 12.6 %all-to-all-start.2 = ((bf16[16,8,1152]{2,1,0:T(8,128)(2,1)}), bf16[16,8,1152]{2,1,0:T(8,128)(2,1)S(1)}, u32[]{:S(2)}, u32[]{:S(2)}) async-start(bf16[16,8,1152]{2,1,0:T(8,128)(2,1)} %get-tuple-element.42), calls=%async_computation.2 | async-start | bytes 589824 | tf_op jit(solution)/shard_map/all_to_all | solution.py:147
  115.9 10.4 %collective-permute-start.18 = (bf16[96,512]{1,0:T(8,128)(2,1)S(1)}, bf16[96,512]{1,0:T(8,128)(2,1)S(1)}, u32[]{:S(2)}, u32[]{:S(2)}) collective-permute-start(bf16[96,512]{1,0:T(8,128)(2,1)S(1)} %get-tuple-element.49), channel_id=1, source_target_pairs={{0,16},{16,32},{32,48},{48,64},{64,80},{80,96},{96,112},{1,17},{17... | collective-permute-start | bytes 294920 | tf_op jit(solution)/shard_map/ppermute | solution.py:118
  118.4 7.9 %collective-permute-start.19 = (bf16[96,512]{1,0:T(8,128)(2,1)S(1)}, bf16[96,512]{1,0:T(8,128)(2,1)S(1)}, u32[]{:S(2)}, u32[]{:S(2)}) collective-permute-start(bf16[96,512]{1,0:T(8,128)(2,1)S(1)} %get-tuple-element.50), channel_id=1, source_target_pairs={{16,0},{32,16},{48,32},{64,48},{80,64},{96,80},{112,96},{17,1},{33... | collective-permute-start | bytes 294920 | tf_op jit(solution)/shard_map/ppermute | solution.py:118
  126.5 14.3 %collective-permute-start.20 = (bf16[80,512]{1,0:T(8,128)(2,1)S(1)}, bf16[80,512]{1,0:T(8,128)(2,1)S(1)}, u32[]{:S(2)}, u32[]{:S(2)}) collective-permute-start(bf16[80,512]{1,0:T(8,128)(2,1)S(1)} %get-tuple-element.65), channel_id=1, source_target_pairs={{0,1},{1,2},{2,3},{3,4},{4,5},{5,6},{6,7},{7,8},{8,9},{9,10},{10,1... | collective-permute-start | bytes 245768 | tf_op jit(solution)/shard_map/ppermute | solution.py:118
  128.4 12.4 %collective-permute-start.21 = (bf16[80,512]{1,0:T(8,128)(2,1)S(1)}, bf16[80,512]{1,0:T(8,128)(2,1)S(1)}, u32[]{:S(2)}, u32[]{:S(2)}) collective-permute-start(bf16[80,512]{1,0:T(8,128)(2,1)S(1)} %get-tuple-element.66), channel_id=1, source_target_pairs={{1,0},{2,1},{3,2},{4,3},{5,4},{6,5},{7,6},{8,7},{9,8},{10,9},{11,1... | collective-permute-start | bytes 245768 | tf_op jit(solution)/shard_map/ppermute | solution.py:118
